TPU v7x, 32 devices: a whole 2x2x4 slice. The times are simulated.
32 devices in a mesh: group: 4 (over x, core), seq: 2 (over y), tp: 4 (over z).
Axes of the slice: x: 2, y: 2, z: 4, core: 2. Of those that a mesh axis runs over, the one named last changes fastest.
Arguments:
- hidden: bfloat16 [2048, 5120], P(('group', 'seq')), may hold values from -6 to 6
- norm_gain: bfloat16 [5120], replicated, may hold values from 0.5 to 1.5
- gen_value: bfloat16 [5120, 2560], P('seq', 'tp'), may hold values from -0.078125 to 0.078125
- gen_head: bfloat16 [2560, 64], P('tp'), may hold values from -0.125 to 0.125
- critic_embed: bfloat16 [2, 64, 5120], replicated, may hold values from -0.75 to 0.75
- critic_gain: bfloat16 [2, 5120], replicated, may hold values from 0.5 to 1.5
- critic_value: bfloat16 [5120, 5120], P('seq', ('group', 'tp')), may hold values from -0.078125 to 0.078125
- critic_head: bfloat16 [5120, 64], P(('group', 'tp')), may hold values from -0.125 to 0.125
- noise: bfloat16 [2048, 64], P('seq'), may hold values from -6 to 6
- owner: int32 [2048], P(('group', 'seq')), may hold values from 0 to 2047, as said below
- tsteps: int32 [1], replicated, may hold values from 0 to 999
- noise_mix: float32 [2, 1000], replicated, may hold values from 0.3 to 1
- gap_weight: float32 [1000], replicated, may hold values from 2 to 16
Outputs:
- gen_latent: bfloat16 [2048, 64], P(('group', 'seq'))
- grad_hidden: bfloat16 [2048, 5120], P(('group', 'seq'), 'tp')
Inputs may be any that keep to these rules, and one draw needn't show every extreme that they name: owner is a permutation of the token positions. The 256 tokens of one generator block (aligned blocks of 256) place at most 255 tokens in one critic position block (aligned blocks of 1024 positions), and exactly 255 in some; every critic position block receives tokens from every generator block.
All inputs are finite; a program needn't handle non-finite values.
Results may differ from a plain program's by a relative error of at most 0.035.
Values may be sent and summed in bfloat16 or wider, within the bound.
A program may use at most 128 MiB of HBM per device.

v0:
```python
import jax
import jax.numpy as jnp
from jax import lax
from jax.sharding import PartitionSpec as P

FTOK = 2048


def gelu_tanh(v):
    return jax.nn.gelu(v, approximate=True)


def local(
    hidden,
    norm_gain,
    gen_value,
    gen_head,
    critic_embed,
    critic_gain,
    critic_value,
    critic_head,
    noise,
    owner,
    tsteps,
    noise_mix,
    gap_weight,
):
    rows = hidden.shape[0]
    width = hidden.shape[1]
    latent_width = gen_head.shape[1]
    seq_count = lax.axis_size("seq")
    group_count = lax.axis_size("group")
    crit_rows = noise.shape[0]
    capacity = 2 * (rows // seq_count) - 1
    group_id = lax.axis_index("group")
    shard_id = group_id * seq_count + lax.axis_index("seq")
    critic_id = group_id // 2
    sign = jnp.where(critic_id == 1, 1.0, -1.0).astype(jnp.float32)
    inputs = hidden.astype(jnp.float32)
    inverse = lax.rsqrt(jnp.mean(inputs * inputs, axis=-1, keepdims=True) + 1e-06)
    gain = norm_gain.astype(jnp.float32)
    normed = (inputs * inverse * gain).astype(jnp.bfloat16)
    gen_full, critic_full = (
        lax.all_gather(gen_value, "seq", axis=0, tiled=True),
        lax.all_gather(critic_value, "seq", axis=0, tiled=True),
    )
    values = jnp.dot(normed, gen_full, preferred_element_type=jnp.float32)
    activated, gelu_back = jax.vjp(gelu_tanh, values)
    latent_part = jnp.dot(
        activated.astype(jnp.bfloat16), gen_head, preferred_element_type=jnp.float32
    )
    gen_latent = lax.psum(latent_part.astype(jnp.bfloat16), "tp")
    target = owner // crit_rows
    order = jnp.argsort(target, stable=True)
    sorted_target = target[order]
    counts = jnp.sum(
        (target[:, None] == jnp.arange(seq_count, dtype=jnp.int32)[None, :]).astype(jnp.int32),
        axis=0,
    )
    starts = jnp.cumsum(counts) - counts
    ranks = jnp.arange(rows, dtype=jnp.int32) - starts[sorted_target]
    slots = jnp.full((seq_count, capacity), -1, jnp.int32).at[sorted_target, ranks].set(order)
    filled = slots >= 0
    safe = jnp.maximum(slots, 0)
    send_rows = jnp.where(filled[..., None], gen_latent[safe], jnp.zeros((), jnp.bfloat16))
    send_place = jnp.where(filled, owner[safe] % crit_rows, crit_rows)
    send_frame = (shard_id * rows + safe) // FTOK
    got_rows, got_place, got_frame = (
        lax.all_to_all(
            jnp.tile(send_rows, (group_count, 1, 1)),
            ("group", "seq"),
            split_axis=0,
            concat_axis=0,
            tiled=True,
        ),
        lax.all_to_all(
            jnp.tile(send_place, (group_count, 1)),
            ("group", "seq"),
            split_axis=0,
            concat_axis=0,
            tiled=True,
        ),
        lax.all_to_all(
            jnp.tile(send_frame, (group_count, 1)),
            ("group", "seq"),
            split_axis=0,
            concat_axis=0,
            tiled=True,
        ),
    )
    flat_place = got_place.reshape(-1)
    placed = (
        jnp.zeros((crit_rows, latent_width), jnp.float32)
        .at[flat_place]
        .set(got_rows.reshape(-1, latent_width).astype(jnp.float32), mode="drop")
    )
    frame_at = (
        jnp.zeros((crit_rows,), jnp.int32).at[flat_place].set(got_frame.reshape(-1), mode="drop")
    )
    level_pick = (
        tsteps[:, None] == jnp.arange(noise_mix.shape[1], dtype=jnp.int32)[None, :]
    ).astype(jnp.float32)
    table = jnp.stack([noise_mix[0], noise_mix[1], gap_weight], axis=1)
    per_frame = jnp.dot(level_pick, table, precision=lax.Precision.HIGHEST)
    frame_pick = (
        frame_at[:, None] == jnp.arange(tsteps.shape[0], dtype=jnp.int32)[None, :]
    ).astype(jnp.float32)
    per_row = jnp.dot(frame_pick, per_frame, precision=lax.Precision.HIGHEST)
    noisy = (per_row[:, 0:1] * placed + per_row[:, 1:2] * noise.astype(jnp.float32)).astype(
        jnp.bfloat16
    )
    embed = lax.dynamic_index_in_dim(critic_embed, critic_id, 0, keepdims=False)
    critic_scale = lax.dynamic_index_in_dim(critic_gain, critic_id, 0, keepdims=False).astype(
        jnp.float32
    )
    block = min(512, crit_rows)
    pieces = []
    for start in range(0, crit_rows, block):
        embedded = jnp.dot(noisy[start : start + block], embed, preferred_element_type=jnp.float32)
        scale_rows = lax.rsqrt(jnp.mean(embedded * embedded, axis=-1, keepdims=True) + 1e-06)
        pieces.append((embedded * scale_rows * critic_scale).astype(jnp.bfloat16))
    critic_normed = jnp.concatenate(pieces, axis=0)
    critic_values = jnp.dot(critic_normed, critic_full, preferred_element_type=jnp.float32)
    critic_act = gelu_tanh(critic_values).astype(jnp.bfloat16)
    term = jnp.dot(critic_act, critic_head, preferred_element_type=jnp.float32) * sign
    gap = lax.psum(term.astype(jnp.bfloat16), ("group", "tp")).astype(jnp.float32)
    pull = (per_row[:, 2:3] * gap).astype(jnp.bfloat16)
    mine = lax.dynamic_slice_in_dim(got_place, group_id * seq_count, seq_count, 0)
    back_rows = jnp.where(
        (mine < crit_rows)[..., None],
        pull[jnp.minimum(mine, crit_rows - 1)],
        jnp.zeros((), jnp.bfloat16),
    )
    returned = lax.all_to_all(back_rows, "seq", split_axis=0, concat_axis=0, tiled=True)
    landing = jnp.where(filled, slots, rows).reshape(-1)
    cotangent = (
        jnp.zeros((rows, latent_width), jnp.bfloat16)
        .at[landing]
        .set(returned.reshape(-1, latent_width), mode="drop")
    )
    grad_act = lax.dot_general(
        cotangent, gen_head, (((1,), (1,)), ((), ())), preferred_element_type=jnp.float32
    )
    grad_values = gelu_back(grad_act)[0].astype(jnp.bfloat16)
    grad_part = lax.dot_general(
        grad_values, gen_full, (((1,), (1,)), ((), ())), preferred_element_type=jnp.float32
    )
    columns_dev = width // lax.axis_size("tp")
    first_col = lax.axis_index("tp") * columns_dev
    grad_normed = lax.psum(grad_part.astype(jnp.bfloat16), "tp").astype(jnp.float32)
    scaled = grad_normed * gain
    mixed = jnp.mean(inputs * scaled, axis=-1, keepdims=True)
    grad_in = inverse * scaled - inputs * inverse * inverse * inverse * mixed
    grad_hidden = lax.dynamic_slice_in_dim(grad_in, first_col, columns_dev, 1).astype(jnp.bfloat16)
    return (gen_latent, grad_hidden)


def solution(mesh):
    return jax.shard_map(
        local,
        mesh=mesh,
        in_specs=(
            P(("group", "seq"), None),
            P(),
            P("seq", "tp"),
            P("tp", None),
            P(),
            P(),
            P("seq", ("group", "tp")),
            P(("group", "tp"), None),
            P("seq", None),
            P(("group", "seq")),
            P(),
            P(),
            P(),
        ),
        out_specs=(P(("group", "seq"), None), P(("group", "seq"), "tp")),
        check_vma=False,
    )
```

profile of v0, /device:TPU:0, one launch (start us, length us, event | category | flops | bytes accessed | tf_op | source)
XLA Modules:
  0.0 384.6 jit_solution(10014979989491108196)
XLA Ops:
  7.2 0.7 all-gather.3.cloned.1.call-update
  8.0 0.7 and_select_fusion.2
  8.7 3.2 sort.17
  11.9 1.9 gather_fusion
  13.8 0.1 fusion.63
  14.0 0.2 reduce-window.9
  14.1 0.6 fusion.90
  14.7 1.3 or_select_fusion
  16.1 12.5 %scatter_fusion = s32[2,255]{1,0:T(2,128)S(1)} fusion(s32[2,255]{1,0:T(2,128)S(1)} %broadcast_in_dim.36, s32[256]{0:T(256)S(1)} %bitcast.49, s32[256]{0:T(256)S(1)} %get-tuple-element.3), kind=kCustom, calls=%fused_computation.4 | custom fusion | bytes 5120 | tf_op jit(solution)/shard_map/scatter | solution.py:62
  28.6 0.1 reshape.246
  28.7 3.5 gather_fusion.1
  32.2 0.1 reshape.245
  32.3 0.6 all_to_all.18
  32.9 5.2 %all-to-all-start = ((s32[8,1,255]{2,1,0:T(1,128)}), s32[8,1,255]{2,1,0:T(1,128)S(1)}, u32[]{:S(2)}, u32[]{:S(2)}) async-start(s32[8,1,255]{2,1,0:T(1,128)} %all_to_all.18), calls=%async_computation | async-start | bytes 16384 | tf_op jit(solution)/shard_map/all_to_all | solution.py:76
  38.1 0.7 all-gather.5.cloned.1.call-update
  39.6 2.3 fusion.4
  42.0 0.1 convolution_bitcast_fusion
  42.1 0.6 all_to_all.20
  42.8 0.2 copy.58
  43.0 0.1 reshape.221
  43.0 4.2 %all-to-all-start.1 = ((s32[8,1,255]{2,1,0:T(1,128)}), s32[8,1,255]{2,1,0:T(1,128)S(1)}, u32[]{:S(2)}, u32[]{:S(2)}) async-start(s32[8,1,255]{2,1,0:T(1,128)} %all_to_all.20), calls=%async_computation.1 | async-start | bytes 16384 | tf_op jit(solution)/shard_map/all_to_all | solution.py:83
  47.3 0.1 reshape.222
  47.4 4.5 %all-to-all-done.1 = s32[8,1,255]{2,1,0:T(1,128)S(1)} async-done(((s32[8,1,255]{2,1,0:T(1,128)}), s32[8,1,255]{2,1,0:T(1,128)S(1)}, u32[]{:S(2)}, u32[]{:S(2)}) %all-to-all-start.1) | async-done | bytes 8192 | tf_op jit(solution)/shard_map/all_to_all | solution.py:83
  51.9 0.1 reshape.278
  52.0 9.9 %scatter_custom_fusion.1 = s32[1024]{0:T(1024)S(1)} fusion(s32[2040]{0:T(1024)S(1)} %bitcast.54, s32[2040]{0:T(1024)S(1)} %reshape.278, s32[]{:T(128)} %constant.72.clone.1), kind=kCustom, calls=%fused_computation.120 | custom fusion | bytes 4100 | tf_op jit(solution)/shard_map/scatter | solution.py:98
  62.0 0.1 broadcast_multiply_fusion
  62.1 33.8 %all-gather.3.cloned.1.call-done = bf16[5120,640]{1,0:T(8,128)(2,1)} async-done(((bf16[2560,640]{1,0:T(8,128)(2,1)}), bf16[5120,640]{1,0:T(8,128)(2,1)}) %all-gather.3.cloned.1.call-update) | async-done | bytes 6553616 | tf_op jit(solution)/shard_map/all_gather | solution.py:44
  95.9 5.9 %fusion.6 = f32[256,640]{1,0:T(8,128)S(1)} fusion(bf16[5120,640]{1,0:T(8,128)(2,1)} %all-gather.3.cloned.1.call-done, f32[5120]{0:T(1024)S(1)} %convert_element_type.65, bf16[256,5120]{1,0:T(8,128)(2,1)} %param.13, f32[256]{0:T(256)S(1)} %add_rsqrt_fusion.2), kind=kOutput, calls=%fused_computation.24 | convolution fusion | flops 1682964480 | bytes 9851904 | tf_op jit(solution)/shard_map/dot_general | solution.py:47
  101.8 0.3 convolution_convert_fusion.1
  102.1 19.0 %psum.21 = bf16[256,64]{0,1:T(8,128)(2,1)S(1)} all-reduce(bf16[256,64]{0,1:T(8,128)(2,1)S(1)} %convolution_convert_fusion.1), channel_id=1, replica_groups=mesh['group'=4,'seq'=2,'tp'=4] {'tp'}, use_global_device_ids=true, to_apply=%region_1.2 | all-reduce | flops 16384 | bytes 65536 | tf_op jit(solution)/shard_map/psum | solution.py:52
  121.1 0.1 copy.53
  121.3 1.3 gather_fusion.2
  122.6 0.1 copy.54
  122.7 0.1 reshape.253
  122.8 0.1 broadcast_select_fusion
  122.9 0.7 tile.10
  123.6 3.4 all-to-all-start.2
  127.0 0.0 all-reduce.3.cloned.1.call-start
  127.2 0.1 reshape.262
  127.3 6.9 %all-to-all-done.2 = bf16[8,255,64]{1,2,0:T(8,128)(2,1)S(1)} async-done(((bf16[8,255,64]{1,2,0:T(8,128)(2,1)}), bf16[8,255,64]{1,2,0:T(8,128)(2,1)S(1)}, u32[]{:S(2)}, u32[]{:S(2)}) %all-to-all-start.2) | async-done | bytes 261152 | tf_op jit(solution)/shard_map/all_to_all | solution.py:69
  134.2 0.2 copy.64
  134.4 1.1 reshape.314
  135.5 8.4 %scatter_custom_fusion.2 = f32[1024,64]{1,0:T(8,128)S(1)} fusion(s32[2040]{0:T(1024)S(1)} %bitcast.55, f32[2040,64]{1,0:T(8,128)} %reshape.314, f32[]{:T(128)} %constant.52.clone.1), kind=kCustom, calls=%fused_computation.75 | custom fusion | bytes 262656 | tf_op jit(solution)/shard_map/scatter | solution.py:95
  143.9 0.3 add_convert_fusion
  144.3 1.6 multiply_reduce_fusion
  145.9 1.6 multiply_reduce_fusion.1
  147.5 5.9 %multiply_convert_fusion.1 = (bf16[512,5120]{1,0:T(8,128)(2,1)}, bf16[512,5120]{1,0:T(8,128)(2,1)}) fusion(f32[512,5120]{1,0:T(8,128)S(1)} %get-tuple-element.20, f32[5120]{0:T(1024)S(1)} %bitcast.50, f32[512]{0:T(512)S(1)} %get-tuple-element.24, f32[512,5120]{1,0:T(8,128)S(1)} %get-tuple-element.22, f32[512]{0:T(512)S(1)} %get-tuple-element.23), kind=kLoop, calls=%fused_computation.14 | loop fusion | flops 15728640 | bytes 31481856 | tf_op jit(solution)/shard_map/convert_element_type | solution.py:121
  153.4 9.7 %fusion.20 = bf16[1024,64]{0,1:T(8,128)(2,1)} fusion(bf16[320,64]{0,1:T(8,128)(2,1)S(1)} %copy-done.9, bf16[5120,320]{0,1:T(8,128)(2,1)} %all-gather.5.cloned.1.call-done, bf16[512,5120]{1,0:T(8,128)(2,1)} %get-tuple-element.8, bf16[512,5120]{1,0:T(8,128)(2,1)} %get-tuple-element.7, f32[]{:T(128)S(6)} %select_n.124), kind=kOutput, calls=%fused_computation.42 | convolution fusion | flops 3421437952 | bytes 13934596 | tf_op jit(solution)/shard_map/dot_general | solution.py:125
  163.1 84.6 %all-reduce.3.cloned.1.call-done = bf16[1024,64]{0,1:T(8,128)(2,1)} async-done(((bf16[1024,64]{0,1:T(8,128)(2,1)}), bf16[1024,64]{0,1:T(8,128)(2,1)}) %all-reduce.3.cloned.1.call-update) | async-done | bytes 131088 | tf_op jit(solution)/shard_map/psum | solution.py:126
  247.7 0.9 multiply_convert_fusion.6
  248.6 0.2 copy.59
  248.8 1.3 gather_fusion.3
  250.1 0.1 copy.60
  250.2 0.1 reshape.261
  250.3 0.1 broadcast_select_fusion.1
  250.4 0.6 copy.61
  251.0 3.3 all-to-all-start.3
  254.4 4.0 %all-to-all-done.3 = bf16[2,255,64]{1,2,0:T(8,128)(2,1)S(1)} async-done(((bf16[2,255,64]{1,2,0:T(8,128)(2,1)}), bf16[2,255,64]{1,2,0:T(8,128)(2,1)S(1)}, u32[]{:S(2)}, u32[]{:S(2)}) %all-to-all-start.3) | async-done | bytes 65312 | tf_op jit(solution)/shard_map/all_to_all | solution.py:134
  258.4 0.1 copy.65
  258.6 2.0 scatter_custom_fusion.3
  260.6 7.0 %convolution_convert_fusion = bf16[256,5120]{1,0:T(8,128)(2,1)} fusion(bf16[5120,640]{1,0:T(8,128)(2,1)} %all-gather.3.cloned.1.call-done, f32[256,640]{1,0:T(8,128)S(1)} %copy-done.12, bf16[256,64]{1,0:T(8,128)(2,1)S(1)} %scatter_custom_fusion.3, bf16[640,64]{0,1:T(8,128)(2,1)S(1)} %copy-done.8), kind=kOutput, calls=%fused_computation.19 | convolution fusion | flops 1703280640 | bytes 9945088 | tf_op jit(solution)/shard_map/dot_general | solution.py:145
  267.6 105.0 %all-reduce.5.cloned.1.call-done = bf16[256,5120]{1,0:T(8,128)(2,1)} async-done(((bf16[256,5120]{1,0:T(8,128)(2,1)}), bf16[256,5120]{1,0:T(8,128)(2,1)}) %all-reduce.5.cloned.1.call-update) | async-done | bytes 2621456 | tf_op jit(solution)/shard_map/psum | solution.py:150
  372.6 4.2 %fusion.5 = (f32[256]{0:T(256)S(1)}, f32[256,5120]{1,0:T(8,128)S(1)}, f32[256,5120]{1,0:T(8,128)S(1)}) fusion(bf16[256,5120]{1,0:T(8,128)(2,1)} %param.13, f32[5120]{0:T(1024)S(1)} %convert_element_type.65, bf16[256,5120]{1,0:T(8,128)(2,1)} %all-reduce.5.cloned.1.call-done, f32[256]{0:T(256)S(1)} %add_rsqrt_fusion.2), kind=kLoop, calls=%fused_computation.21 | loop fusion | flops 7864064 | bytes 15751168 | tf_op jit(solution)/shard_map/reduce_sum | solution.py:152
  376.9 1.2 fusion.17
  (64 shorter events, 0.5 us)
Async XLA Ops:
  7.2 137.1 %copy-start = (bf16[2,64,5120]{2,1,0:T(8,128)(2,1)S(1)}, bf16[2,64,5120]{2,1,0:T(8,128)(2,1)}, u32[]{:S(2)}) copy-start(bf16[2,64,5120]{2,1,0:T(8,128)(2,1)} %param.17) | copy-start | bytes 3932164
  7.2 21.5 %copy-start.2 = (s32[256]{0:T(256)S(1)}, s32[256]{0:T(256)}, u32[]{:S(2)}) copy-start(s32[256]{0:T(256)} %param.22) | copy-start | bytes 3076
  7.2 31.7 %copy-start.7 = (f32[2,1000]{1,0:T(2,128)S(1)}, f32[2,1000]{1,0:T(2,128)}, u32[]{:S(2)}) copy-start(f32[2,1000]{1,0:T(2,128)} %param.24) | copy-start | bytes 24004
  7.2 88.6 %all-gather.3.cloned.1.call-start = ((), (), s32[]{:S(2)}) async-start(), calls=%async_computation.4 | async-start | bytes 9830400 | tf_op jit(solution)/shard_map/all_gather | solution.py:44
  7.9 34.0 %copy-start.5 = (bf16[2,5120]{1,0:T(2,128)(2,1)S(1)}, bf16[2,5120]{1,0:T(2,128)(2,1)}, u32[]{:S(2)}) copy-start(bf16[2,5120]{1,0:T(2,128)(2,1)} %param.18) | copy-start | bytes 61444
  7.9 34.0 %copy-start.10 = (f32[1000]{0:T(1024)S(1)}, f32[1000]{0:T(1024)}, u32[]{:S(2)}) copy-start(f32[1000]{0:T(1024)} %param.25) | copy-start | bytes 12004
  8.0 34.8 %copy-start.6 = (bf16[5120]{0:T(1024)(128)(2,1)S(1)}, bf16[5120]{0:T(1024)(128)(2,1)}, u32[]{:S(2)}) copy-start(bf16[5120]{0:T(1024)(128)(2,1)} %param.14) | copy-start | bytes 30724
  8.0 34.8 %copy-start.3 = (bf16[1024,64]{0,1:T(8,128)(2,1)S(1)}, bf16[1024,64]{0,1:T(8,128)(2,1)}, u32[]{:S(2)}) copy-start(bf16[1024,64]{0,1:T(8,128)(2,1)} %param.21) | copy-start | bytes 393220
  32.9 10.1 %all-to-all-start = ((s32[8,1,255]{2,1,0:T(1,128)}), s32[8,1,255]{2,1,0:T(1,128)S(1)}, u32[]{:S(2)}, u32[]{:S(2)}) async-start(s32[8,1,255]{2,1,0:T(1,128)} %all_to_all.18), calls=%async_computation | async-start | bytes 16384 | tf_op jit(solution)/shard_map/all_to_all | solution.py:76
  38.1 115.3 %all-gather.5.cloned.1.call-start = ((), (), s32[]{:S(2)}) async-start(), calls=%async_computation.5 | async-start | bytes 4915200 | tf_op jit(solution)/shard_map/all_gather | solution.py:45
  43.0 8.9 %all-to-all-start.1 = ((s32[8,1,255]{2,1,0:T(1,128)}), s32[8,1,255]{2,1,0:T(1,128)S(1)}, u32[]{:S(2)}, u32[]{:S(2)}) async-start(s32[8,1,255]{2,1,0:T(1,128)} %all_to_all.20), calls=%async_computation.1 | async-start | bytes 16384 | tf_op jit(solution)/shard_map/all_to_all | solution.py:83
  62.1 39.7 %copy-start.8 = (bf16[640,64]{0,1:T(8,128)(2,1)S(1)}, bf16[640,64]{0,1:T(8,128)(2,1)}, u32[]{:S(2)}) copy-start(bf16[640,64]{0,1:T(8,128)(2,1)} %param.16) | copy-start | bytes 245764
  101.8 25.5 %copy-start.11 = (f32[256,640]{1,0:T(8,128)}, f32[256,640]{1,0:T(8,128)S(1)}, u32[]{:S(2)}) copy-start(f32[256,640]{1,0:T(8,128)S(1)} %fusion.6) | copy-start | bytes 1966084
  121.1 24.7 %copy-start.4 = (bf16[256,64]{0,1:T(8,128)(2,1)}, bf16[256,64]{0,1:T(8,128)(2,1)S(1)}, u32[]{:S(2)}) copy-start(bf16[256,64]{0,1:T(8,128)(2,1)S(1)} %psum.21) | copy-start | bytes 98308
  123.6 10.5 %all-to-all-start.2 = ((bf16[8,255,64]{1,2,0:T(8,128)(2,1)}), bf16[8,255,64]{1,2,0:T(8,128)(2,1)S(1)}, u32[]{:S(2)}, u32[]{:S(2)}) async-start(bf16[8,255,64]{1,2,0:T(8,128)(2,1)} %bitcast.15), calls=%async_computation.2 | async-start | bytes 524288 | tf_op jit(solution)/shard_map/all_to_all | solution.py:69
  127.0 120.6 %all-reduce.3.cloned.1.call-start = ((), (), s32[]{:S(2)}) async-start(), calls=%async_computation.6 | async-start | bytes 262144 | tf_op jit(solution)/shard_map/psum | solution.py:126
  147.5 5.9 %copy-start.9 = (bf16[320,64]{0,1:T(8,128)(2,1)S(1)}, bf16[320,64]{0,1:T(8,128)(2,1)}, u32[]{:S(2)}) copy-start(bf16[320,64]{0,1:T(8,128)(2,1)} %param.20) | copy-start | bytes 122884
  153.4 107.2 %copy-start.12 = (f32[256,640]{1,0:T(8,128)S(1)}, f32[256,640]{1,0:T(8,128)}, u32[]{:S(2)}) copy-start(f32[256,640]{1,0:T(8,128)} %copy-done.11) | copy-start | bytes 1966084
  251.0 7.4 %all-to-all-start.3 = ((bf16[2,255,64]{1,2,0:T(8,128)(2,1)}), bf16[2,255,64]{1,2,0:T(8,128)(2,1)S(1)}, u32[]{:S(2)}, u32[]{:S(2)}) async-start(bf16[2,255,64]{1,2,0:T(8,128)(2,1)} %copy.61), calls=%async_computation.3 | async-start | bytes 131072 | tf_op jit(solution)/shard_map/all_to_all | solution.py:134
  254.3 118.3 %all-reduce.5.cloned.1.call-start = ((), (), s32[]{:S(2)}) async-start(), calls=%async_computation.7 | async-start | bytes 5242880 | tf_op jit(solution)/shard_map/psum | solution.py:150
  372.6 5.4 %copy-start.1 = (bf16[2,64,5120]{2,1,0:T(8,128)(2,1)S(1)}, bf16[2,64,5120]{2,1,0:T(8,128)(2,1)}, u32[]{:S(2)}) copy-start(bf16[2,64,5120]{2,1,0:T(8,128)(2,1)} %param.17) | copy-start | bytes 3932164
Sparse Core Ops, SparseCore 0:
  9.6 86.2 all-gather.2
  97.4 49.2 all-gather.4
  163.2 84.4 all-reduce.2
  267.7 104.8 all-reduce.4
where the time goes:
time: 385 us
  waiting for transfers between devices  240 us (62%)
  local copies, waits for them, and re-layouts  47.1 us (12%)
  matrix products  26.3 us (7%)
  other arithmetic  20.8 us (5%)
  blocking collectives  19 us (5%)
  starting transfers between devices  16.2 us (4%)
  between operations  14.9 us (4%)
    psum x1, waiting for transfers between devices, local(): lax.psum(grad_part.astype(jnp.bfloat16), 'tp').astype(jnp.float32)  105 us
    psum x1, waiting for transfers between devices, local(): lax.psum(term.astype(jnp.bfloat16), ('group', 'tp')).astype(jnp.float32)  84.6 us
    all_gather x1, waiting for transfers between devices, local(): lax.all_gather(gen_value, 'seq', axis=0, tiled=True)  33.8 us
    psum x1, blocking collectives, local(): gen_latent = lax.psum(latent_part.astype(jnp.bfloat16), 'tp')  19 us
    scatter x1, local copies, waits for them, and re-layouts, local(): jnp.full((seq_count, capacity), -1, jnp.int32).at[sorted_target, ranks]  12.5 us
    scatter x1, local copies, waits for them, and re-layouts, local(): jnp.zeros((crit_rows,), jnp.int32).at[flat_place]  9.93 us
    dot_general x1, matrix products, local(): jnp.dot(critic_act, critic_head, preferred_element_type=jnp.float32) * sign  9.68 us
    scatter x1, local copies, waits for them, and re-layouts, local(): placed = jnp.zeros((crit_rows, latent_width), jnp.float32).at[flat_place]...  8.44 us
  transfers between devices with their start and end apart: 8, of which 6 were waited for; matrix products, arithmetic and copies ran while one was open for 17% of the time, Pallas kernels for 0%

commit v1 on v0

v1 whole, which is shorter than its diff:
```python
import jax
import jax.numpy as jnp
from jax import lax
from jax.sharding import PartitionSpec as P

FTOK = 2048


def gelu_tanh(v):
    return jax.nn.gelu(v, approximate=True)


def split_bf16(v):
    hi = lax.reduce_precision(v, 8, 7)
    return hi.astype(jnp.bfloat16), (v - hi).astype(jnp.bfloat16)


def local(
    hidden,
    norm_gain,
    gen_value,
    gen_head,
    critic_embed,
    critic_gain,
    critic_value,
    critic_head,
    noise,
    owner,
    tsteps,
    noise_mix,
    gap_weight,
):
    f32 = jnp.float32
    rows, width = hidden.shape
    depth = gen_value.shape[0]
    seq_count = lax.axis_size("seq")
    group_count = lax.axis_size("group")
    tp_count = lax.axis_size("tp")
    group_id = lax.axis_index("group")
    seq_id = lax.axis_index("seq")
    tp_id = lax.axis_index("tp")
    critic_id = group_id // (group_count // 2)
    frame = ((group_id * seq_count + seq_id) * rows) // FTOK
    level = lax.dynamic_index_in_dim(tsteps, frame, 0, keepdims=False)
    mix = lax.dynamic_index_in_dim(noise_mix, level, 1, keepdims=False)
    weight = lax.dynamic_index_in_dim(gap_weight, level, 0, keepdims=False)

    gen_full = lax.all_gather(gen_value, "seq", axis=0, tiled=True)
    noise_rows = lax.all_gather(noise, "seq", axis=0, tiled=True)[owner].astype(f32)

    first = seq_id * depth
    embed = lax.dynamic_slice(critic_embed, (critic_id, 0, first), (1, critic_embed.shape[1], depth))[0]
    gains = lax.dynamic_slice(critic_gain, (critic_id, first), (1, depth))
    eg_hi, eg_lo = split_bf16(embed.astype(f32) * gains.astype(f32))
    folded = jnp.dot(eg_hi, critic_value, preferred_element_type=f32) + jnp.dot(
        eg_lo, critic_value, preferred_element_type=f32
    )
    folded = lax.psum(folded, "seq")
    m_hi, m_lo = split_bf16(folded)
    m_pair = jnp.concatenate([m_hi, m_lo], axis=0)
    m_all = lax.all_gather(m_pair, "group", axis=0, tiled=False)
    head_all = lax.all_gather(critic_head, "group", axis=0, tiled=False)

    inputs = hidden.astype(f32)
    inverse = lax.rsqrt(jnp.mean(inputs * inputs, axis=-1, keepdims=True) + 1e-06)
    gain = norm_gain.astype(f32)
    normed = (inputs * inverse * gain).astype(jnp.bfloat16)
    values = jnp.dot(normed, gen_full, preferred_element_type=f32)
    activated, gelu_back = jax.vjp(gelu_tanh, values)
    latent_part = jnp.dot(activated.astype(jnp.bfloat16), gen_head, preferred_element_type=f32)
    gen_latent = lax.psum(latent_part.astype(jnp.bfloat16), "tp")

    noisy = (mix[0] * gen_latent.astype(f32) + mix[1] * noise_rows).astype(jnp.bfloat16)
    noisy32 = noisy.astype(f32)
    pair = jnp.concatenate([noisy, noisy], axis=1)
    scales = []
    for which in range(2):
        gram = lax.dot_general(
            critic_embed[which], critic_embed[which], (((1,), (1,)), ((), ())), preferred_element_type=f32
        )
        quad = jnp.sum(jnp.dot(noisy32, gram, precision=lax.Precision.HIGHEST) * noisy32, axis=-1, keepdims=True)
        scales.append(lax.rsqrt(jnp.maximum(quad, 0.0) / width + 1e-06))
    gap = 0.0
    for member in range(group_count):
        which = member // (group_count // 2)
        crit = jnp.dot(pair, m_all[member], preferred_element_type=f32) * scales[which]
        term = jnp.dot(gelu_tanh(crit).astype(jnp.bfloat16), head_all[member], preferred_element_type=f32)
        gap = gap + term if which else gap - term
    gap = lax.psum(gap.astype(jnp.bfloat16), "tp").astype(f32)
    cotangent = (weight * gap).astype(jnp.bfloat16)

    grad_act = lax.dot_general(cotangent, gen_head, (((1,), (1,)), ((), ())), preferred_element_type=f32)
    grad_values = gelu_back(grad_act)[0].astype(jnp.bfloat16)
    inner = jnp.sum(grad_values.astype(f32) * values, axis=-1, keepdims=True)
    mixed = lax.psum(inner, "tp") / (inverse * width)
    grad_part = lax.dot_general(grad_values, gen_full, (((1,), (1,)), ((), ())), preferred_element_type=f32)
    grad_normed = lax.psum_scatter(grad_part.astype(jnp.bfloat16), "tp", scatter_dimension=1, tiled=True)
    columns = width // tp_count
    own = lax.dynamic_slice_in_dim(hidden, tp_id * columns, columns, 1).astype(f32)
    own_gain = lax.dynamic_slice_in_dim(gain, tp_id * columns, columns, 0)
    scaled = grad_normed.astype(f32) * own_gain
    grad_hidden = inverse * scaled - own * inverse * inverse * inverse * mixed
    return (gen_latent, grad_hidden.astype(jnp.bfloat16))


def solution(mesh):
    return jax.shard_map(
        local,
        mesh=mesh,
        in_specs=(
            P(("group", "seq"), None),
            P(),
            P("seq", "tp"),
            P("tp", None),
            P(),
            P(),
            P("seq", ("group", "tp")),
            P(("group", "tp"), None),
            P("seq", None),
            P(("group", "seq")),
            P(),
            P(),
            P(),
        ),
        out_specs=(P(("group", "seq"), None), P(("group", "seq"), "tp")),
        check_vma=False,
    )
```

time: 385 us -> 236 us (0.61)
  waiting for transfers between devices: 240 us -> 118 us
  blocking collectives: 19 us -> 68.3 us
  local copies, waits for them, and re-layouts: 47.1 us -> 4.39 us
  starting transfers between devices: 16.2 us -> 0.12 us
  other arithmetic: 20.8 us -> 8.19 us
  matrix products: 26.3 us -> 20.9 us
    psum x2 -> x1, waiting for transfers between devices: 190 us -> 0.02 us  [local(): folded = lax.psum(folded, 'seq')]
    all_gather x2 -> x1, waiting for transfers between devices: 33.8 us -> 77.2 us  [local(): gen_full = lax.all_gather(gen_value, 'seq', axis=0, tiled=True)]
    reduce_scatter x0 -> x1, waiting for transfers between devices: none -> 40.5 us  [local(): lax.psum_scatter(grad_part.astype(jnp.bfloat16), 'tp', scatter_dimension=...]
    scatter x4 -> x0, local copies, waits for them, and re-layouts: 32.9 us -> none  [the longest x1 12.5 us: local(): jnp.full((seq_count, capacity), -1, jnp.int32).at[sorted_target, ranks]]
    psum x0 -> x2, blocking collectives: none -> 26 us  [the longest x1 15.8 us: local(): gap = lax.psum(gap.astype(jnp.bfloat16), 'tp').astype(f32)]
    all_gather x0 -> x3, blocking collectives: none -> 23.3 us  [the longest x1 11 us: local(): lax.all_gather(noise, 'seq', axis=0, tiled=True)[owner].astype(f32)]
    all_to_all x4 -> x0, starting transfers between devices: 16.1 us -> none  [the longest x1 5.17 us: local(): lax.all_to_all(jnp.tile(send_place, (group_count, 1)), ('group', 'seq'),...]
    all_to_all x4 -> x0, waiting for transfers between devices: 15.5 us -> none  [the longest x1 6.91 us: local(): lax.all_to_all(jnp.tile(send_rows, (group_count, 1, 1)), ('group', 'seq')...]
  transfers between devices with their start and end apart: 8 -> 3, of which waited for: 6 -> 2; matrix products, arithmetic and copies ran while one was open for 17% -> 3% of each run, Pallas kernels for 0% -> 0%
where the time goes in v1:
time: 236 us; the launch traced here: 235 us
  waiting for transfers between devices  118 us (50%)
  blocking collectives  68.3 us (29%)
  matrix products  20.9 us (9%)
  between operations  14.7 us (6%)
  other arithmetic  8.19 us (3%)
  local copies, waits for them, and re-layouts  4.39 us (2%)
    all_gather x1, waiting for transfers between devices, local(): gen_full = lax.all_gather(gen_value, 'seq', axis=0, tiled=True)  77.2 us
    reduce_scatter x1, waiting for transfers between devices, local(): lax.psum_scatter(grad_part.astype(jnp.bfloat16), 'tp', scatter_dimension=...  40.5 us
    psum x1, blocking collectives, local(): gen_latent = lax.psum(latent_part.astype(jnp.bfloat16), 'tp')  19 us
    psum x1, blocking collectives, local(): gap = lax.psum(gap.astype(jnp.bfloat16), 'tp').astype(f32)  15.8 us
    all_gather x1, blocking collectives, local(): lax.all_gather(noise, 'seq', axis=0, tiled=True)[owner].astype(f32)  11 us
    psum x1, blocking collectives, local(): mixed = lax.psum(inner, 'tp') / (inverse * width)  10.3 us
    all_gather x1, blocking collectives, local(): m_all = lax.all_gather(m_pair, 'group', axis=0, tiled=False)  6.68 us
    dot_general x1, matrix products, local(): lax.dot_general(grad_values, gen_full, (((1,), (1,)), ((), ())), preferre...  6.66 us
  transfers between devices with their start and end apart: 3, of which 2 were waited for; matrix products, arithmetic and copies ran while one was open for 3% of the time, Pallas kernels for 0%

profile of v1, /device:TPU:0, one launch (start us, length us, event | category | flops | bytes accessed | tf_op | source)
XLA Modules:
  0.0 235.0 jit_solution(6429251791447045363)
XLA Ops:
  7.2 0.0 copy-start
  7.2 0.0 all-reduce.2.cloned.1.call-start
  7.2 0.9 convert_reduce_fusion
  8.2 0.4 copy-done
  8.6 1.6 fusion.57
  10.2 2.2 convolution_add_fusion
  12.4 0.0 all-reduce.2.cloned.1.call-update
  12.4 0.0 copy-start.5
  12.5 0.0 copy-start.2
  12.5 0.0 copy-start.6
  12.5 0.0 all-gather.5.cloned.1.call-start
  12.5 0.7 all-gather.5.cloned.1.call-update
  13.2 0.0 copy-start.4
  13.2 0.0 reduce-scatter.2.cloned.1.call-start
  13.9 0.0 copy-done.5
  14.0 0.0 copy-done.2
  14.0 0.2 copy.19
  14.2 11.0 %all_gather.19 = bf16[2048,64]{1,0:T(8,128)(2,1)S(1)} all-gather(bf16[1024,64]{1,0:T(8,128)(2,1)S(1)} %copy.19), channel_id=1, replica_groups=mesh['group'=4,'seq'=2,'tp'=4] {'seq'}, dimensions={0}, use_global_device_ids=true | all-gather | bytes 393216 | tf_op jit(solution)/shard_map/all_gather | solution.py:49
  25.1 0.0 copy-done.6
  25.2 0.9 gather_fusion
  26.0 0.0 copy-start.1
  26.0 0.1 copy.20
  26.1 1.3 dynamic_slice.22
  27.5 0.0 copy-done.4
  27.5 5.6 %all-gather.2 = bf16[4,320,64]{1,2,0:T(8,128)(2,1)S(1)} all-gather(bf16[1,320,64]{1,2,0:T(8,128)(2,1)S(1)} %bitcast.50), channel_id=3, replica_groups=mesh['group'=4,'seq'=2,'tp'=4] {'group'}, dimensions={0}, use_global_device_ids=true | all-gather | bytes 204800 | tf_op jit(solution)/shard_map/all_gather | solution.py:62
  33.1 0.8 constant_dynamic-slice_fusion
  33.8 0.6 fusion.124
  34.4 2.3 fusion
  36.8 0.0 copy-done.1
  36.8 0.3 fusion.20
  37.1 0.3 fusion.18
  37.4 0.0 all-reduce.2.cloned.1.call-done
  37.5 0.9 reduce-precision_convert_fusion.2
  38.4 6.7 %all-gather = bf16[512,320]{1,0:T(8,128)(2,1)S(1)} all-gather(bf16[128,320]{1,0:T(8,128)(2,1)S(1)} %pad_maximum_fusion), channel_id=2, replica_groups=mesh['group'=4,'seq'=2,'tp'=4] {'group'}, dimensions={0}, use_global_device_ids=true | all-gather | bytes 409600 | tf_op jit(solution)/shard_map/all_gather | solution.py:61
  45.1 77.2 %all-gather.5.cloned.1.call-done = bf16[5120,640]{1,0:T(8,128)(2,1)} async-done(((bf16[2560,640]{1,0:T(8,128)(2,1)}), bf16[5120,640]{1,0:T(8,128)(2,1)}) %all-gather.5.cloned.1.call-update) | async-done | bytes 6553616 | tf_op jit(solution)/shard_map/all_gather | solution.py:48
  122.3 0.0 copy-start.7
  122.3 5.9 %fusion.3 = f32[256,640]{1,0:T(8,128)S(1)} fusion(bf16[5120,640]{1,0:T(8,128)(2,1)} %all-gather.5.cloned.1.call-done, bf16[256,5120]{1,0:T(8,128)(2,1)} %param.13, f32[5120]{0:T(1024)S(1)} %convert_element_type.86, f32[256]{0:T(256)S(1)} %get-tuple-element.5), kind=kOutput, calls=%fused_computation.7 | convolution fusion | flops 1682964480 | bytes 9851904 | tf_op jit(solution)/shard_map/dot_general | solution.py:68
  128.3 0.0 copy-done.7
  128.3 0.3 convolution_convert_fusion.1
  128.6 19.0 %psum.28 = bf16[256,64]{0,1:T(8,128)(2,1)S(1)} all-reduce(bf16[256,64]{0,1:T(8,128)(2,1)S(1)} %convolution_convert_fusion.1), channel_id=1, replica_groups=mesh['group'=4,'seq'=2,'tp'=4] {'tp'}, use_global_device_ids=true, to_apply=%region_1.2 | all-reduce | flops 16384 | bytes 65536 | tf_op jit(solution)/shard_map/psum | solution.py:71
  147.6 0.0 copy-start.3
  147.6 1.4 add_convert_fusion
  149.0 0.2 fusion.8
  149.3 0.4 convolution_subtract_fusion.1
  149.7 0.4 convolution_subtract_fusion
  150.2 0.2 fusion.9
  150.4 0.4 convolution_add_fusion.2
  150.9 0.0 copy-done.3
  150.9 0.4 fusion.7
  151.3 15.8 %psum.30 = bf16[256,64]{0,1:T(8,128)(2,1)S(1)} all-reduce(bf16[256,64]{0,1:T(8,128)(2,1)S(1)} %fusion.7), channel_id=1, replica_groups=mesh['group'=4,'seq'=2,'tp'=4] {'tp'}, use_global_device_ids=true, to_apply=%region_5.6 | all-reduce | flops 16384 | bytes 65536 | tf_op jit(solution)/shard_map/psum | solution.py:89
  167.1 1.3 multiply_reduce_fusion
  168.4 6.7 %convolution_convert_fusion = bf16[256,5120]{1,0:T(8,128)(2,1)} fusion(bf16[256,640]{1,0:T(8,128)(2,1)S(1)} %get-tuple-element.9, bf16[5120,640]{1,0:T(8,128)(2,1)} %all-gather.5.cloned.1.call-done), kind=kOutput, calls=%fused_computation.3 | convolution fusion | flops 1679032320 | bytes 9502720 | tf_op jit(solution)/shard_map/dot_general | solution.py:96
  175.0 0.0 reduce-scatter.2.cloned.1.call-update
  175.0 0.1 dynamic_slice.26
  175.1 10.3 %psum.31 = f32[256,1]{0,1:T(1,128)S(1)} all-reduce(f32[256,1]{0,1:T(1,128)S(1)} %bitcast.53), channel_id=1, replica_groups=mesh['group'=4,'seq'=2,'tp'=4] {'tp'}, use_global_device_ids=true, to_apply=%region_8.9 | all-reduce | flops 256 | bytes 2048 | tf_op jit(solution)/shard_map/psum | solution.py:95
  185.4 40.5 %reduce-scatter.2.cloned.1.call-done = bf16[256,1280]{1,0:T(8,128)(2,1)} async-done(((bf16[256,5120]{1,0:T(8,128)(2,1)}), bf16[256,1280]{1,0:T(8,128)(2,1)}) %reduce-scatter.2.cloned.1.call-update) | async-done | bytes 655376 | tf_op jit(solution)/shard_map/reduce_scatter | solution.py:97
  225.9 2.6 %subtract_convert_fusion = bf16[256,1280]{1,0:T(8,128)(2,1)} fusion(bf16[256,1280]{1,0:T(8,128)(2,1)} %reduce-scatter.2.cloned.1.call-done, f32[256]{0:T(256)S(1)} %bitcast.51, bf16[256,5120]{1,0:T(8,128)(2,1)} %param.13, s32[]{:T(128)S(6)} %select_n.34, f32[1280]{0:T(1024)S(1)} %dynamic_slice.26, f32[256]{0:T(256)S(1)} %get-tuple-element.5), kind=kLoop, calls=%fused_computation.10 | loop fusion | flops 3276800 | bytes 1973252 | tf_op jit(solution)/shard_map/convert_element_type | solution.py:103
  (8 shorter events, 0.1 us)
Async XLA Ops:
  7.2 1.5 copy-start
  7.2 30.3 %all-reduce.2.cloned.1.call-start = ((), (), s32[]{:S(2)}) async-start(), calls=%async_computation.2 | async-start | bytes 196608 | tf_op jit(solution)/shard_map/psum | solution.py:58
  12.4 1.5 copy-start.5
  12.5 1.5 copy-start.2
  12.5 12.7 %copy-start.6 = (s32[256]{0:T(256)S(1)}, s32[256]{0:T(256)}, u32[]{:S(2)}) copy-start(s32[256]{0:T(256)} %param.22) | copy-start | bytes 3076
  12.5 109.8 %all-gather.5.cloned.1.call-start = ((), (), s32[]{:S(2)}) async-start(), calls=%async_computation.1 | async-start | bytes 9830400 | tf_op jit(solution)/shard_map/all_gather | solution.py:48
  13.2 14.2 %copy-start.4 = (bf16[320,64]{0,1:T(8,128)(2,1)S(1)}, bf16[320,64]{0,1:T(8,128)(2,1)}, u32[]{:S(2)}) copy-start(bf16[320,64]{0,1:T(8,128)(2,1)} %param.20) | copy-start | bytes 122884
  13.2 212.7 %reduce-scatter.2.cloned.1.call-start = ((), (), s32[]{:S(2)}) async-start(), calls=%async_computation.3 | async-start | bytes 3276800 | tf_op jit(solution)/shard_map/reduce_scatter | solution.py:97
  26.0 10.8 %copy-start.1 = (bf16[2,64,5120]{2,1,0:T(8,128)(2,1)S(1)}, bf16[2,64,5120]{2,1,0:T(8,128)(2,1)}, u32[]{:S(2)}) copy-start(bf16[2,64,5120]{2,1,0:T(8,128)(2,1)} %param.17) | copy-start | bytes 3932164
  122.3 6.0 %copy-start.7 = (bf16[640,64]{0,1:T(8,128)(2,1)S(1)}, bf16[640,64]{0,1:T(8,128)(2,1)}, u32[]{:S(2)}) copy-start(bf16[640,64]{0,1:T(8,128)(2,1)} %param.16) | copy-start | bytes 245764
  147.6 3.3 %copy-start.3 = (bf16[256,64]{0,1:T(8,128)(2,1)}, bf16[256,64]{0,1:T(8,128)(2,1)S(1)}, u32[]{:S(2)}) copy-start(bf16[256,64]{0,1:T(8,128)(2,1)S(1)} %psum.28) | copy-start | bytes 98308
Sparse Core Ops, SparseCore 0:
  12.6 24.7 all-reduce.1
  38.9 83.3 all-gather.4
  175.2 50.6 reduce-scatter.1

commit v2 on v1

v2 whole, which is shorter than its diff:
```python
import functools
import jax
import jax.numpy as jnp
from jax import lax
from jax.experimental import pallas as pl
from jax.experimental.pallas import tpu as pltpu
from jax.sharding import PartitionSpec as P

FTOK = 2048
MESH = pl.DeviceIdType.MESH
F32 = jnp.float32
BF16 = jnp.bfloat16
ROOT = 0.7978845608028654
CUBE = 0.044715


def split_bf16(v):
    hi = lax.reduce_precision(v, 8, 7)
    return hi.astype(BF16), (v - hi).astype(BF16)


def gelu_tanh(v):
    return 0.5 * v * (1.0 + jnp.tanh(ROOT * (v + CUBE * v * v * v)))


def dot(a, b):
    return jnp.dot(a, b, preferred_element_type=F32)


def dot_t(a, b):
    return lax.dot_general(a, b, (((1,), (1,)), ((), ())), preferred_element_type=F32)


def kernel(
    ng, ns, nt, shared, pieces,
    hidden, gain, weights, gen_head, embed, eg_pair, crit_value, crit_head, noise, owner, coef,
    latent_out, grad_out,
    wall, normed, inv_ref, values, slope, mpart, mall, hall, noise_all, latp, gapp, inn,
    send_r, send_l, recv_r, recv_l, total,
    own_sem, w_send, w_recv, f_send, f_recv, m_send, m_recv, n_send, n_recv,
    g_send, g_recv, h_send, h_recv, t_send, t_recv, rs_sem, rr_sem, ls_sem, lr_sem,
):
    g = lax.axis_index("group")
    s = lax.axis_index("seq")
    t = lax.axis_index("tp")
    rows, width = hidden.shape
    depth = weights.shape[0]
    crit_rows = noise.shape[0]
    columns = width // nt
    pending = []

    def seq_peer(o):
        return lax.rem(s + o, ns)

    def group_peer(o):
        return lax.rem(g + o, ng)

    def tp_peer(o):
        return lax.rem(t + o, nt)

    def push(src, dst, send, recv, where):
        copy = pltpu.make_async_remote_copy(
            src_ref=src, dst_ref=dst, send_sem=send, recv_sem=recv,
            device_id=where, device_id_type=MESH,
        )
        copy.start()
        pending.append(copy)
        return copy

    barrier = pltpu.get_barrier_semaphore()
    for o in range(1, ns):
        pl.semaphore_signal(barrier, inc=1, device_id={"seq": seq_peer(o)}, device_id_type=MESH)
    for o in range(1, ng):
        pl.semaphore_signal(barrier, inc=1, device_id={"group": group_peer(o)}, device_id_type=MESH)
    for o in range(1, nt):
        pl.semaphore_signal(barrier, inc=1, device_id={"tp": tp_peer(o)}, device_id_type=MESH)
    pl.semaphore_wait(barrier, ns + ng + nt - 3)

    local = pltpu.make_async_copy(weights, wall.at[pl.ds(s * depth, depth), :], own_sem)
    local.start()
    quarter = depth // ng if shared else depth
    step = quarter // pieces
    mine = g * quarter if shared else 0
    w_copies = {}
    for p in range(pieces):
        for o in range(1, ns):
            w_copies[o, p] = push(
                weights.at[pl.ds(mine + p * step, step), :],
                wall.at[pl.ds(s * depth + mine + p * step, step), :],
                w_send.at[o - 1, p], w_recv.at[o - 1, p], {"seq": seq_peer(o)},
            )
    n_copies = [
        push(noise, noise_all.at[s], n_send.at[o - 1], n_recv.at[o - 1], {"seq": seq_peer(o)})
        for o in range(1, ns)
    ]
    h_copies = [
        push(crit_head, hall.at[g], h_send.at[o - 1], h_recv.at[o - 1], {"group": group_peer(o)})
        for o in range(1, ng)
    ]
    noise_all[s] = noise[...]
    hall[g] = crit_head[...]

    folded = dot(eg_pair[...], crit_value[...])
    half = folded.shape[0] // 2
    mpart[s] = folded[:half] + folded[half:]
    m_copies = [
        push(mpart.at[s], mpart.at[s], m_send.at[o - 1], m_recv.at[o - 1], {"seq": seq_peer(o)})
        for o in range(1, ns)
    ]

    def norm_rows(r, carry):
        at = pl.ds(pl.multiple_of(r * 32, 32), 32)
        x = hidden[at, :].astype(F32)
        inverse = lax.rsqrt(jnp.mean(x * x, axis=-1, keepdims=True) + 1e-06)
        normed[at, :] = (x * inverse * gain[...].astype(F32)).astype(BF16)
        inv_ref[at, :] = jnp.broadcast_to(inverse, (32, 128))
        return carry

    lax.fori_loop(0, rows // 32, norm_rows, 0)
    values[...] = jnp.zeros_like(values)

    def add_rows(start, size):
        at = pl.multiple_of(start, 128)
        values[...] += dot(normed[:, pl.ds(at, size)], wall[pl.ds(at, size), :])

    if shared:
        x_copies, c_copies, d_copies = {}, {}, {}
        for p in range(pieces):
            for o in range(1, ns):
                w_copies[o, p].wait_recv()
                base = lax.rem(s - o + ns, ns) * depth
                at = pl.ds(base + mine + p * step, step)
                x_copies[o, p] = push(
                    wall.at[at, :], wall.at[at, :],
                    f_send.at[0, o - 1, p], f_recv.at[0, o - 1, p], {"group": g ^ 2},
                )
                c_copies[o, p] = push(
                    wall.at[at, :], wall.at[at, :],
                    f_send.at[1, o - 1, p], f_recv.at[1, o - 1, p], {"group": g ^ 1},
                )
            if p == 0:
                local.wait()

                def own_rows(j, carry):
                    add_rows(s * depth + j * quarter, quarter)
                    return carry

                lax.fori_loop(0, ng, own_rows, 0)
        for p in range(pieces):
            for o in range(1, ns):
                x_copies[o, p].wait_recv()
                base = lax.rem(s - o + ns, ns) * depth
                at = pl.ds(base + (g ^ 2) * quarter + p * step, step)
                d_copies[o, p] = push(
                    wall.at[at, :], wall.at[at, :],
                    f_send.at[2, o - 1, p], f_recv.at[2, o - 1, p], {"group": g ^ 1},
                )
    else:
        local.wait()

    for copy in m_copies:
        copy.wait_recv()
    whole = mpart[0]
    for k in range(1, ns):
        whole = whole + mpart[k]
    high = whole.astype(BF16)
    mall[g, :half] = high
    mall[g, half:] = (whole - high.astype(F32)).astype(BF16)
    g_copies = [
        push(mall.at[g], mall.at[g], g_send.at[o - 1], g_recv.at[o - 1], {"group": group_peer(o)})
        for o in range(1, ng)
    ]
    grams = []
    for which in range(2):
        gram = dot_t(embed[which], embed[which])
        first = gram.astype(BF16)
        rest = gram - first.astype(F32)
        second = rest.astype(BF16)
        grams.append((first, second, (rest - second.astype(F32)).astype(BF16)))
    for copy in n_copies:
        copy.wait_recv()

    def pick(k, carry):
        place = lax.broadcasted_iota(jnp.int32, (rows, crit_rows), 1) + k * crit_rows
        hot = (place == owner[...]).astype(F32).astype(BF16)
        return carry + dot(hot, noise_all[k])

    noise_rows = lax.fori_loop(0, ns, pick, jnp.zeros((rows, noise.shape[1]), F32))

    if shared:
        for o in range(1, ns):
            base = lax.rem(s - o + ns, ns) * depth
            add_rows(base + g * quarter, quarter)
            add_rows(base + (g ^ 2) * quarter, quarter)
            for p in range(pieces):
                c_copies[o, p].wait_recv()
            add_rows(base + (g ^ 1) * quarter, quarter)
            for p in range(pieces):
                d_copies[o, p].wait_recv()
            add_rows(base + (g ^ 3) * quarter, quarter)
    else:
        for copy in w_copies.values():
            copy.wait_recv()

        def all_rows(j, carry):
            add_rows(j * (width // 8), width // 8)
            return carry

        lax.fori_loop(0, 8, all_rows, 0)

    def share_tp(buffer, index):
        return [
            push(buffer.at[t], buffer.at[t], t_send.at[index, o - 1], t_recv.at[index, o - 1], {"tp": tp_peer(o)})
            for o in range(1, nt)
        ]

    def sum_tp(buffer, copies):
        for copy in copies:
            copy.wait_recv()
        out = buffer[0].astype(F32)
        for k in range(1, nt):
            out = out + buffer[k].astype(F32)
        return out

    v = values[...]
    tanh = jnp.tanh(ROOT * (v + CUBE * v * v * v))
    latp[t] = dot((0.5 * v * (1.0 + tanh)).astype(BF16), gen_head[...]).astype(BF16)
    lat_copies = share_tp(latp, 0)
    slope[...] = 0.5 * (1.0 + tanh) + 0.5 * v * (1.0 - tanh * tanh) * ROOT * (1.0 + 3.0 * CUBE * v * v)
    for copy in g_copies + h_copies:
        copy.wait_recv()
    latent = sum_tp(latp, lat_copies).astype(BF16)
    latent_out[...] = latent

    noisy = (coef[:, 0:1] * latent.astype(F32) + coef[:, 1:2] * noise_rows).astype(BF16)
    noisy32 = noisy.astype(F32)
    scales = []
    for which in range(2):
        a, b, c = grams[which]
        quad = jnp.sum((dot(noisy, a) + dot(noisy, b) + dot(noisy, c)) * noisy32, axis=-1, keepdims=True)
        scales.append(lax.rsqrt(jnp.maximum(quad, 0.0) / width + 1e-06))
    pair = jnp.concatenate([noisy, noisy], axis=1)
    gap = jnp.zeros((rows, noise.shape[1]), F32)
    for member in range(ng):
        which = member // (ng // 2)
        act = gelu_tanh(dot(pair, mall[member]) * scales[which]).astype(BF16)
        term = dot(act, hall[member])
        gap = gap + term if which else gap - term
    gapp[t] = gap.astype(BF16)
    gap = sum_tp(gapp, share_tp(gapp, 1))
    cotangent = (coef[:, 2:3] * gap).astype(BF16)

    grad_values = (slope[...] * dot_t(cotangent, gen_head[...])).astype(BF16)
    inner = jnp.sum(grad_values.astype(F32) * values[...], axis=-1, keepdims=True)
    inn[t] = jnp.broadcast_to(inner, (rows, 128)).T[:8]
    inn_copies = share_tp(inn, 2)

    block = 256 if columns % 256 == 0 else columns

    def part(q, out, extra):
        def one(j, carry):
            at = pl.ds(pl.multiple_of(j * block, block), block)
            w = wall[pl.ds(pl.multiple_of(q * columns + j * block, block), block), :]
            term = dot_t(grad_values, w)
            if extra is not None:
                term = term + extra[:, at].astype(F32)
            out[:, at] = term.astype(out.dtype)
            return carry

        lax.fori_loop(0, columns // block, one, 0)

    def chain(d, to_right):
        buf_s, buf_r = (send_r, recv_r) if to_right else (send_l, recv_l)
        sem_s, sem_r = (rs_sem, rr_sem) if to_right else (ls_sem, lr_sem)
        target = t + d if to_right else t - d
        inside = target <= nt - 1 if to_right else target >= 0
        starts = t == 0 if to_right else t == nt - 1
        neighbour = {"tp": t + 1 if to_right else t - 1}

        def link(k):
            return pltpu.make_async_remote_copy(
                src_ref=buf_s.at[k], dst_ref=buf_r.at[k], send_sem=sem_s.at[k], recv_sem=sem_r.at[k],
                device_id=neighbour, device_id_type=MESH,
            )

        @pl.when(inside)
        def _():
            if d < nt - 1:
                @pl.when(starts)
                def _():
                    part(target, buf_s.at[d - 1], None)
                    link(d).wait_send()

                @pl.when(jnp.logical_not(starts))
                def _():
                    link(d).wait_recv()
                    part(target, buf_s.at[d - 1], buf_r.at[d])
                    if d < nt - 2:
                        @pl.when(target + 1 <= nt - 1 if to_right else target - 1 >= 0)
                        def _():
                            link(d).wait_send()
            else:
                part(target, buf_s.at[d - 1], None)
            link(d - 1).start()

    def chain_end(to_right):
        buf_s, buf_r = (send_r, recv_r) if to_right else (send_l, recv_l)
        sem_s, sem_r = (rs_sem, rr_sem) if to_right else (ls_sem, lr_sem)
        neighbour = {"tp": t + 1 if to_right else t - 1}
        link = pltpu.make_async_remote_copy(
            src_ref=buf_s.at[0], dst_ref=buf_r.at[0], send_sem=sem_s.at[0], recv_sem=sem_r.at[0],
            device_id=neighbour, device_id_type=MESH,
        )

        @pl.when(t > 0 if to_right else t < nt - 1)
        def _():
            link.wait_recv()
            total[...] += buf_r[0].astype(F32)

        @pl.when(t < nt - 1 if to_right else t > 0)
        def _():
            link.wait_send()

    for d in range(nt - 1, 0, -1):
        chain(d, True)
        chain(d, False)
    part(t, total, None)
    inner_all = sum_tp(inn, inn_copies)
    inner_col = jnp.broadcast_to(inner_all[0:1], (128, rows)).T[:, :1]
    chain_end(True)
    chain_end(False)
    inverse = inv_ref[:, :1]
    mixed = inner_col / (inverse * width)
    factor = inverse * inverse * inverse * mixed

    def finish(j, carry):
        at = pl.ds(pl.multiple_of(j * block, block), block)
        far = pl.ds(pl.multiple_of(t * columns + j * block, block), block)
        scaled = total[:, at] * gain[:, far].astype(F32)
        grad_out[:, at] = (inverse * scaled - hidden[:, far].astype(F32) * factor).astype(BF16)
        return carry

    lax.fori_loop(0, columns // block, finish, 0)
    for copy in pending:
        copy.wait_send()


def local(
    hidden,
    norm_gain,
    gen_value,
    gen_head,
    critic_embed,
    critic_gain,
    critic_value,
    critic_head,
    noise,
    owner,
    tsteps,
    noise_mix,
    gap_weight,
):
    rows, width = hidden.shape
    depth, heads = gen_value.shape
    crit_rows, latent_width = noise.shape
    crit_cols = critic_value.shape[1]
    ns = lax.axis_size("seq")
    ng = lax.axis_size("group")
    nt = lax.axis_size("tp")
    group_id = lax.axis_index("group")
    seq_id = lax.axis_index("seq")
    critic_id = group_id // (ng // 2)
    frame = ((group_id * ns + seq_id) * rows) // FTOK
    level = lax.dynamic_index_in_dim(tsteps, frame, 0, keepdims=False)
    mix = lax.dynamic_index_in_dim(noise_mix, level, 1, keepdims=False)
    weight = lax.dynamic_index_in_dim(gap_weight, level, 0, keepdims=True)
    coef = jnp.pad(jnp.concatenate([mix, weight]), (0, 125)).reshape(1, 128)
    first = seq_id * depth
    embed = lax.dynamic_slice(critic_embed, (critic_id, 0, first), (1, latent_width, depth))[0]
    gains = lax.dynamic_slice(critic_gain, (critic_id, first), (1, depth))
    eg_pair = jnp.concatenate(split_bf16(embed.astype(F32) * gains.astype(F32)), axis=0)

    shared = ng == 4 and depth % (128 * ng) == 0
    pieces = 4 if shared else 1
    vmem = pl.BlockSpec(memory_space=pltpu.VMEM)
    columns = width // nt
    dma = pltpu.SemaphoreType.DMA
    return pl.pallas_call(
        functools.partial(kernel, ng, ns, nt, shared, pieces),
        out_shape=(
            jax.ShapeDtypeStruct((rows, latent_width), BF16),
            jax.ShapeDtypeStruct((rows, columns), BF16),
        ),
        in_specs=[vmem, vmem, pl.BlockSpec(memory_space=pl.ANY)] + [vmem] * 8,
        out_specs=(vmem, vmem),
        scratch_shapes=[
            pltpu.VMEM((width, heads), BF16),
            pltpu.VMEM((rows, width), BF16),
            pltpu.VMEM((rows, 128), F32),
            pltpu.VMEM((rows, heads), F32),
            pltpu.VMEM((rows, heads), F32),
            pltpu.VMEM((ns, latent_width, crit_cols), F32),
            pltpu.VMEM((ng, 2 * latent_width, crit_cols), BF16),
            pltpu.VMEM((ng, crit_cols, latent_width), BF16),
            pltpu.VMEM((ns, crit_rows, latent_width), BF16),
            pltpu.VMEM((nt, rows, latent_width), BF16),
            pltpu.VMEM((nt, rows, latent_width), BF16),
            pltpu.VMEM((nt, 8, rows), F32),
            pltpu.VMEM((nt - 1, rows, columns), BF16),
            pltpu.VMEM((nt - 1, rows, columns), BF16),
            pltpu.VMEM((nt - 1, rows, columns), BF16),
            pltpu.VMEM((nt - 1, rows, columns), BF16),
            pltpu.VMEM((rows, columns), F32),
            dma,
            dma((ns - 1, pieces)),
            dma((ns - 1, pieces)),
            dma((3, ns - 1, pieces)),
            dma((3, ns - 1, pieces)),
            dma((ns - 1,)),
            dma((ns - 1,)),
            dma((ns - 1,)),
            dma((ns - 1,)),
            dma((ng - 1,)),
            dma((ng - 1,)),
            dma((ng - 1,)),
            dma((ng - 1,)),
            dma((3, nt - 1)),
            dma((3, nt - 1)),
            dma((nt - 1,)),
            dma((nt - 1,)),
            dma((nt - 1,)),
            dma((nt - 1,)),
        ],
        compiler_params=pltpu.CompilerParams(
            collective_id=0, has_side_effects=True, vmem_limit_bytes=56 * 1024 * 1024
        ),
    )(
        hidden, norm_gain.reshape(1, width), gen_value, gen_head, critic_embed, eg_pair,
        critic_value, critic_head, noise, owner.reshape(rows, 1), coef,
    )


def solution(mesh):
    return jax.shard_map(
        local,
        mesh=mesh,
        in_specs=(
            P(("group", "seq"), None),
            P(),
            P("seq", "tp"),
            P("tp", None),
            P(),
            P(),
            P("seq", ("group", "tp")),
            P(("group", "tp"), None),
            P("seq", None),
            P(("group", "seq")),
            P(),
            P(),
            P(),
        ),
        out_specs=(P(("group", "seq"), None), P(("group", "seq"), "tp")),
        check_vma=False,
    )
```

time: 236 us -> 121 us (0.51)
  waiting for transfers between devices: 118 us -> 0 us
  Pallas kernels: 0 us -> 99.7 us
  blocking collectives: 68.3 us -> 0 us
  matrix products: 20.9 us -> 0 us
  between operations: 14.7 us -> 1.33 us
  local copies, waits for them, and re-layouts: 4.39 us -> 15.3 us
  other arithmetic: 8.19 us -> 3.99 us
    pallas_call x0 -> x1, Pallas kernels: none -> 99.7 us  [local(): pl.pallas_call(functools.partial(kernel, ng, ns, nt, shared, pieces), out...]
    all_gather x1 -> x0, waiting for transfers between devices: 77.2 us -> none  [local(): gen_full = lax.all_gather(gen_value, 'seq', axis=0, tiled=True)]
    psum x3 -> x0, blocking collectives: 45 us -> none  [the longest x1 19 us: local(): gen_latent = lax.psum(latent_part.astype(jnp.bfloat16), 'tp')]
    reduce_scatter x1 -> x0, waiting for transfers between devices: 40.5 us -> none  [local(): lax.psum_scatter(grad_part.astype(jnp.bfloat16), 'tp', scatter_dimension=...]
    all_gather x3 -> x0, blocking collectives: 23.3 us -> none  [the longest x1 11 us: local(): lax.all_gather(noise, 'seq', axis=0, tiled=True)[owner].astype(f32)]
    dot_general x14 -> x0, matrix products: 20.9 us -> none  [the longest x1 6.66 us: local(): lax.dot_general(grad_values, gen_full, (((1,), (1,)), ((), ())), preferre...]
    unnamed x17 -> x9, local copies, waits for them, and re-layouts: 0.66 us -> 9.5 us
    convert_element_type x4 -> x1, other arithmetic: 4.87 us -> 1.08 us  [split_bf16(): return (hi.astype(BF16), (v - hi).astype(BF16))]
  transfers between devices with their start and end apart: 3 -> 0, of which waited for: 2 -> 0; matrix products, arithmetic and copies ran while one was open for 3% -> 0% of each run, Pallas kernels for 0% -> 0%
where the time goes in v2:
time: 121 us; the launch traced here: 120 us
  Pallas kernels  99.7 us (82%)
  local copies, waits for them, and re-layouts  15.3 us (13%)
  other arithmetic  3.99 us (3%)
  between operations  1.33 us (1%)
    pallas_call x1, Pallas kernels, local(): pl.pallas_call(functools.partial(kernel, ng, ns, nt, shared, pieces), out...  99.7 us
    unnamed x9, local copies, waits for them, and re-layouts  9.5 us

profile of v2, /device:TPU:0, one launch (start us, length us, event | category | flops | bytes accessed | tf_op | source)
XLA Modules:
  0.0 120.3 jit_solution(15547074537685398794)
XLA Ops:
  0.6 0.0 copy-start
  1.3 1.3 %dynamic_slice.19 = f32[1]{0:T(128)} dynamic-slice(f32[1000]{0:T(1024)} %param.25, s32[]{:T(128)S(6)} %select_n.25), dynamic_slice_sizes={1} | dynamic-slice | bytes 12 | tf_op jit(solution)/shard_map/jit(dynamic_index_in_dim)/dynamic_slice | solution.py:376
  2.6 0.0 copy-done
  2.6 0.2 dynamic-slice_reduce_fusion
  2.8 1.2 %fusion.2.coef = f32[1,128]{1,0:T(1,128)} fusion(f32[1]{0:T(128)} %dynamic_slice.19, f32[2]{0:T(128)S(1)} %dynamic-slice_reduce_fusion), kind=kLoop, calls=%fused_computation.10 | loop fusion | flops 512 | bytes 524 | tf_op jit(solution)/shard_map/reshape | solution.py:377
  4.0 0.8 convert_reduce_fusion
  4.8 1.3 %reshape.15.gain = bf16[1,5120]{1,0:T(2,128)(2,1)} reshape(bf16[5120]{0:T(1024)(128)(2,1)} %param.14) | data formatting | bytes 20480 | tf_op jit(solution)/shard_map/reshape | solution.py:438
  6.1 1.5 %copy.22.crit_head = bf16[320,64]{1,0:T(8,128)(2,1)} copy(bf16[320,64]{0,1:T(8,128)(2,1)} %param.20) | data formatting | bytes 81920 | tf_op args[7]
  7.7 1.5 %copy.24.owner = s32[256,1]{1,0:T(8,128)} copy(s32[256,1]{0,1:T(1,128)} %bitcast.11) | data formatting | bytes 2048 | tf_op jit(solution)/shard_map/reshape | solution.py:439
  9.1 1.7 %copy.20.gen_head = bf16[640,64]{1,0:T(8,128)(2,1)} copy(bf16[640,64]{0,1:T(8,128)(2,1)} %param.16) | data formatting | bytes 163840 | tf_op args[3]
  10.8 0.0 copy-start.1
  10.8 1.9 %copy.23.noise = bf16[1024,64]{1,0:T(8,128)(2,1)} copy(bf16[1024,64]{0,1:T(8,128)(2,1)} %param.21) | data formatting | bytes 262144 | tf_op args[8]
  12.7 1.1 reduce-precision_convert_fusion
  13.8 0.9 pad_maximum_fusion.eg_pair
  14.6 0.0 copy-done.1
  14.7 2.4 %copy.21.crit_value = bf16[2560,320]{1,0:T(8,128)(2,1)} copy(bf16[2560,320]{0,1:T(8,128)(2,1)S(1)} %copy-done.1) | data formatting | bytes 3276800 | tf_op args[6]
  17.1 99.7 %shard_map.140 = (bf16[256,64]{1,0:T(8,128)(2,1)}, bf16[256,1280]{1,0:T(8,128)(2,1)}) custom-call(bf16[256,5120]{1,0:T(8,128)(2,1)} %hidden.1, bf16[1,5120]{1,0:T(2,128)(2,1)} %reshape.15.gain, bf16[2560,640]{1,0:T(8,128)(2,1)} %weights.1, bf16[640,64]{1,0:T(8,128)(2,1)} %copy.20.gen_head, bf16[2,64,5120]{2,1,0:T(8,128)(2,1)} %embed.1, ...), custom_call_target="tpu_custom_call" | custom-call | tf_op jit(solution)/shard_map/pallas_call | solution.py:388
  116.8 1.5 %copy.25 = bf16[256,64]{0,1:T(8,128)(2,1)} copy(bf16[256,64]{1,0:T(8,128)(2,1)} %get-tuple-element.4) | data formatting | bytes 65536 | tf_op jit(solution)/shard_map/pallas_call | solution.py:388
  118.3 2.0 %copy.28 = bf16[256,1280]{1,0:T(8,128)(2,1)} copy(bf16[256,1280]{1,0:T(8,128)(2,1)} %get-tuple-element.11) | data formatting | bytes 1310720
Async XLA Ops:
  0.6 2.0 %copy-start = (f32[2,1000]{1,0:T(2,128)S(1)}, f32[2,1000]{1,0:T(2,128)}, u32[]{:S(2)}) copy-start(f32[2,1000]{1,0:T(2,128)} %param.24) | copy-start | bytes 24004
  10.8 3.8 %copy-start.1 = (bf16[2560,320]{0,1:T(8,128)(2,1)S(1)}, bf16[2560,320]{0,1:T(8,128)(2,1)}, u32[]{:S(2)}) copy-start(bf16[2560,320]{0,1:T(8,128)(2,1)} %param.19) | copy-start | bytes 4915204

commit v3 on v2

--- a/solution.py
+++ b/solution.py
@@ -7,6 +7,7 @@
 from jax.sharding import PartitionSpec as P
 
 FTOK = 2048
+HALVES = 2
 MESH = pl.DeviceIdType.MESH
 F32 = jnp.float32
 BF16 = jnp.bfloat16
@@ -33,9 +34,9 @@
 
 def kernel(
     ng, ns, nt, shared, pieces,
-    hidden, gain, weights, gen_head, embed, eg_pair, crit_value, crit_head, noise, owner, coef,
+    hidden, gain_in, weights, gen_head, embed, scaling, crit_value, crit_head, noise, owner, tsteps, tables, weighting,
     latent_out, grad_out,
-    wall, normed, inv_ref, values, slope, mpart, mall, hall, noise_all, latp, gapp, inn,
+    gain, wall, normed, inv_ref, values, slope, mpart, mall, hall, noise_all, latp, gapp, inn,
     send_r, send_l, recv_r, recv_l, total,
     own_sem, w_send, w_recv, f_send, f_recv, m_send, m_recv, n_send, n_recv,
     g_send, g_recv, h_send, h_recv, t_send, t_recv, rs_sem, rr_sem, ls_sem, lr_sem,
@@ -45,7 +46,8 @@
     t = lax.axis_index("tp")
     rows, width = hidden.shape
     depth = weights.shape[0]
-    crit_rows = noise.shape[0]
+    crit_rows = noise.shape[1]
+    channels = noise.shape[0]
     columns = width // nt
     pending = []
 
@@ -100,19 +102,31 @@
     noise_all[s] = noise[...]
     hall[g] = crit_head[...]
 
-    folded = dot(eg_pair[...], crit_value[...])
-    half = folded.shape[0] // 2
+    half = channels
+    if depth % 128 == 0:
+        critic = g // (ng // 2)
+        at = pl.ds(pl.multiple_of(s * depth, 128), depth)
+        both = scaling[:, at].astype(F32)
+        eg = embed[critic, :, at].astype(F32) * jnp.where(critic == 0, both[0:1], both[1:2])
+        eg_high = eg.astype(BF16)
+        eg_low = (eg - eg_high.astype(F32)).astype(BF16)
+        eg_pair = jnp.concatenate([eg_high, eg_low], axis=0)
+    else:
+        eg_pair = scaling[...]
+    folded = dot_t(eg_pair, crit_value[...])
     mpart[s] = folded[:half] + folded[half:]
     m_copies = [
         push(mpart.at[s], mpart.at[s], m_send.at[o - 1], m_recv.at[o - 1], {"seq": seq_peer(o)})
         for o in range(1, ns)
     ]
 
+    gain[...] = gain_in[...].astype(F32).reshape(1, width)
+
     def norm_rows(r, carry):
         at = pl.ds(pl.multiple_of(r * 32, 32), 32)
         x = hidden[at, :].astype(F32)
         inverse = lax.rsqrt(jnp.mean(x * x, axis=-1, keepdims=True) + 1e-06)
-        normed[at, :] = (x * inverse * gain[...].astype(F32)).astype(BF16)
+        normed[at, :] = (x * inverse * gain[...]).astype(BF16)
         inv_ref[at, :] = jnp.broadcast_to(inverse, (32, 128))
         return carry
 
@@ -164,8 +178,13 @@
     for k in range(1, ns):
         whole = whole + mpart[k]
     high = whole.astype(BF16)
-    mall[g, :half] = high
-    mall[g, half:] = (whole - high.astype(F32)).astype(BF16)
+    high32 = high.astype(F32)
+    cols = whole.shape[1]
+    fill = -cols % 128
+    both = jnp.concatenate([high32, whole - high32], axis=0)
+    if fill:
+        both = jnp.concatenate([both, jnp.zeros((2 * half, fill), F32)], axis=1)
+    mall[g] = both.T[:cols].astype(BF16)
     g_copies = [
         push(mall.at[g], mall.at[g], g_send.at[o - 1], g_recv.at[o - 1], {"group": group_peer(o)})
         for o in range(1, ng)
@@ -181,11 +200,17 @@
         copy.wait_recv()
 
     def pick(k, carry):
-        place = lax.broadcasted_iota(jnp.int32, (rows, crit_rows), 1) + k * crit_rows
-        hot = (place == owner[...]).astype(F32).astype(BF16)
-        return carry + dot(hot, noise_all[k])
-
-    noise_rows = lax.fori_loop(0, ns, pick, jnp.zeros((rows, noise.shape[1]), F32))
+        place = lax.broadcasted_iota(jnp.int32, (crit_rows, rows), 0) + k * crit_rows
+        hot = jnp.where(place == owner_row, 1.0, 0.0).astype(BF16)
+        return carry + dot(noise_all[k], hot)
+
+    owner_row = owner[...].reshape(1, rows)
+    noise_rows = lax.fori_loop(0, ns, pick, jnp.zeros((channels, rows), F32))
+    level = tsteps[((g * ns + s) * rows) // FTOK]
+    levels = tables.shape[1]
+    found = lax.broadcasted_iota(jnp.int32, (1, levels), 1) == level
+    mix = jnp.sum(jnp.where(found, tables[...], 0.0), axis=1, keepdims=True)
+    weight = jnp.sum(jnp.where(found, weighting[...].reshape(1, levels), 0.0), axis=1, keepdims=True)
 
     if shared:
         for o in range(1, ns):
@@ -224,7 +249,7 @@
 
     v = values[...]
     tanh = jnp.tanh(ROOT * (v + CUBE * v * v * v))
-    latp[t] = dot((0.5 * v * (1.0 + tanh)).astype(BF16), gen_head[...]).astype(BF16)
+    latp[t] = dot_t(gen_head[...], (0.5 * v * (1.0 + tanh)).astype(BF16)).astype(BF16)
     lat_copies = share_tp(latp, 0)
     slope[...] = 0.5 * (1.0 + tanh) + 0.5 * v * (1.0 - tanh * tanh) * ROOT * (1.0 + 3.0 * CUBE * v * v)
     for copy in g_copies + h_copies:
@@ -232,36 +257,43 @@
     latent = sum_tp(latp, lat_copies).astype(BF16)
     latent_out[...] = latent
 
-    noisy = (coef[:, 0:1] * latent.astype(F32) + coef[:, 1:2] * noise_rows).astype(BF16)
+    noisy = (mix[0:1] * latent.astype(F32) + mix[1:2] * noise_rows).astype(BF16)
     noisy32 = noisy.astype(F32)
     scales = []
     for which in range(2):
         a, b, c = grams[which]
-        quad = jnp.sum((dot(noisy, a) + dot(noisy, b) + dot(noisy, c)) * noisy32, axis=-1, keepdims=True)
+        quad = jnp.sum((dot(a, noisy) + dot(b, noisy) + dot(c, noisy)) * noisy32, axis=0, keepdims=True)
         scales.append(lax.rsqrt(jnp.maximum(quad, 0.0) / width + 1e-06))
-    pair = jnp.concatenate([noisy, noisy], axis=1)
-    gap = jnp.zeros((rows, noise.shape[1]), F32)
+    pair = jnp.concatenate([noisy, noisy], axis=0)
+    gap = jnp.zeros((channels, rows), F32)
     for member in range(ng):
         which = member // (ng // 2)
-        act = gelu_tanh(dot(pair, mall[member]) * scales[which]).astype(BF16)
-        term = dot(act, hall[member])
+        act = gelu_tanh(dot(mall[member], pair) * scales[which]).astype(BF16)
+        term = dot(hall[member], act)
         gap = gap + term if which else gap - term
     gapp[t] = gap.astype(BF16)
     gap = sum_tp(gapp, share_tp(gapp, 1))
-    cotangent = (coef[:, 2:3] * gap).astype(BF16)
-
-    grad_values = (slope[...] * dot_t(cotangent, gen_head[...])).astype(BF16)
+    pull = weight * gap
+    fill = -channels % 128
+    if fill:
+        pull = jnp.concatenate([pull, jnp.zeros((fill, rows), F32)], axis=0)
+    cotangent = pull.T[:, :channels].astype(BF16)
+
+    grad_values = (slope[...] * dot(cotangent, gen_head[...])).astype(BF16)
     inner = jnp.sum(grad_values.astype(F32) * values[...], axis=-1, keepdims=True)
     inn[t] = jnp.broadcast_to(inner, (rows, 128)).T[:8]
     inn_copies = share_tp(inn, 2)
 
     block = 256 if columns % 256 == 0 else columns
-
-    def part(q, out, extra):
+    part_rows = rows // HALVES
+
+    def part(q, h, out, extra):
+        lhs = grad_values[h * part_rows:(h + 1) * part_rows]
+
         def one(j, carry):
             at = pl.ds(pl.multiple_of(j * block, block), block)
             w = wall[pl.ds(pl.multiple_of(q * columns + j * block, block), block), :]
-            term = dot_t(grad_values, w)
+            term = dot_t(lhs, w)
             if extra is not None:
                 term = term + extra[:, at].astype(F32)
             out[:, at] = term.astype(out.dtype)
@@ -269,66 +301,69 @@
 
         lax.fori_loop(0, columns // block, one, 0)
 
-    def chain(d, to_right):
+    def linker(to_right):
         buf_s, buf_r = (send_r, recv_r) if to_right else (send_l, recv_l)
         sem_s, sem_r = (rs_sem, rr_sem) if to_right else (ls_sem, lr_sem)
+
+        def link(k, h):
+            return pltpu.make_async_remote_copy(
+                src_ref=buf_s.at[k, h], dst_ref=buf_r.at[k, h], send_sem=sem_s.at[k, h], recv_sem=sem_r.at[k, h],
+                device_id={"tp": t + 1 if to_right else t - 1}, device_id_type=MESH,
+            )
+
+        return buf_s, buf_r, link
+
+    def chain(d, h, to_right):
+        buf_s, buf_r, link = linker(to_right)
         target = t + d if to_right else t - d
         inside = target <= nt - 1 if to_right else target >= 0
         starts = t == 0 if to_right else t == nt - 1
-        neighbour = {"tp": t + 1 if to_right else t - 1}
-
-        def link(k):
-            return pltpu.make_async_remote_copy(
-                src_ref=buf_s.at[k], dst_ref=buf_r.at[k], send_sem=sem_s.at[k], recv_sem=sem_r.at[k],
-                device_id=neighbour, device_id_type=MESH,
-            )
+        further = target + 1 <= nt - 1 if to_right else target - 1 >= 0
 
         @pl.when(inside)
         def _():
             if d < nt - 1:
                 @pl.when(starts)
                 def _():
-                    part(target, buf_s.at[d - 1], None)
-                    link(d).wait_send()
+                    part(target, h, buf_s.at[d - 1, h], None)
+                    link(d, h).wait_send()
 
                 @pl.when(jnp.logical_not(starts))
                 def _():
-                    link(d).wait_recv()
-                    part(target, buf_s.at[d - 1], buf_r.at[d])
+                    link(d, h).wait_recv()
+                    part(target, h, buf_s.at[d - 1, h], buf_r.at[d, h])
                     if d < nt - 2:
-                        @pl.when(target + 1 <= nt - 1 if to_right else target - 1 >= 0)
+                        @pl.when(further)
                         def _():
-                            link(d).wait_send()
+                            link(d, h).wait_send()
             else:
-                part(target, buf_s.at[d - 1], None)
-            link(d - 1).start()
-
-    def chain_end(to_right):
-        buf_s, buf_r = (send_r, recv_r) if to_right else (send_l, recv_l)
-        sem_s, sem_r = (rs_sem, rr_sem) if to_right else (ls_sem, lr_sem)
-        neighbour = {"tp": t + 1 if to_right else t - 1}
-        link = pltpu.make_async_remote_copy(
-            src_ref=buf_s.at[0], dst_ref=buf_r.at[0], send_sem=sem_s.at[0], recv_sem=sem_r.at[0],
-            device_id=neighbour, device_id_type=MESH,
-        )
+                part(target, h, buf_s.at[d - 1, h], None)
+            link(d - 1, h).start()
+
+    def chain_end(h, to_right):
+        buf_s, buf_r, link = linker(to_right)
+        at = pl.ds(h * part_rows, part_rows)
 
         @pl.when(t > 0 if to_right else t < nt - 1)
         def _():
-            link.wait_recv()
-            total[...] += buf_r[0].astype(F32)
+            link(0, h).wait_recv()
+            total[at, :] += buf_r[0, h].astype(F32)
 
         @pl.when(t < nt - 1 if to_right else t > 0)
         def _():
-            link.wait_send()
+            link(0, h).wait_send()
 
     for d in range(nt - 1, 0, -1):
-        chain(d, True)
-        chain(d, False)
-    part(t, total, None)
+        for h in range(HALVES):
+            chain(d, h, True)
+            chain(d, h, False)
+    for h in range(HALVES):
+        part(t, h, total.at[pl.ds(h * part_rows, part_rows), :], None)
     inner_all = sum_tp(inn, inn_copies)
     inner_col = jnp.broadcast_to(inner_all[0:1], (128, rows)).T[:, :1]
-    chain_end(True)
-    chain_end(False)
+    for h in range(HALVES):
+        chain_end(h, True)
+        chain_end(h, False)
     inverse = inv_ref[:, :1]
     mixed = inner_col / (inverse * width)
     factor = inverse * inverse * inverse * mixed
@@ -336,7 +371,7 @@
     def finish(j, carry):
         at = pl.ds(pl.multiple_of(j * block, block), block)
         far = pl.ds(pl.multiple_of(t * columns + j * block, block), block)
-        scaled = total[:, at] * gain[:, far].astype(F32)
+        scaled = total[:, at] * gain[:, far]
         grad_out[:, at] = (inverse * scaled - hidden[:, far].astype(F32) * factor).astype(BF16)
         return carry
 
@@ -369,47 +404,47 @@
     nt = lax.axis_size("tp")
     group_id = lax.axis_index("group")
     seq_id = lax.axis_index("seq")
-    critic_id = group_id // (ng // 2)
-    frame = ((group_id * ns + seq_id) * rows) // FTOK
-    level = lax.dynamic_index_in_dim(tsteps, frame, 0, keepdims=False)
-    mix = lax.dynamic_index_in_dim(noise_mix, level, 1, keepdims=False)
-    weight = lax.dynamic_index_in_dim(gap_weight, level, 0, keepdims=True)
-    coef = jnp.pad(jnp.concatenate([mix, weight]), (0, 125)).reshape(1, 128)
-    first = seq_id * depth
-    embed = lax.dynamic_slice(critic_embed, (critic_id, 0, first), (1, latent_width, depth))[0]
-    gains = lax.dynamic_slice(critic_gain, (critic_id, first), (1, depth))
-    eg_pair = jnp.concatenate(split_bf16(embed.astype(F32) * gains.astype(F32)), axis=0)
+    if depth % 128 == 0:
+        scaling = critic_gain
+    else:
+        critic_id = group_id // (ng // 2)
+        first = seq_id * depth
+        embed = lax.dynamic_slice(critic_embed, (critic_id, 0, first), (1, latent_width, depth))[0]
+        gains = lax.dynamic_slice(critic_gain, (critic_id, first), (1, depth))
+        scaling = jnp.concatenate(split_bf16(embed.astype(F32) * gains.astype(F32)), axis=0)
 
     shared = ng == 4 and depth % (128 * ng) == 0
-    pieces = 4 if shared else 1
+    pieces = 8 if shared else 1
     vmem = pl.BlockSpec(memory_space=pltpu.VMEM)
     columns = width // nt
     dma = pltpu.SemaphoreType.DMA
-    return pl.pallas_call(
+    latent, grad = pl.pallas_call(
         functools.partial(kernel, ng, ns, nt, shared, pieces),
         out_shape=(
-            jax.ShapeDtypeStruct((rows, latent_width), BF16),
+            jax.ShapeDtypeStruct((latent_width, rows), BF16),
             jax.ShapeDtypeStruct((rows, columns), BF16),
         ),
-        in_specs=[vmem, vmem, pl.BlockSpec(memory_space=pl.ANY)] + [vmem] * 8,
+        in_specs=[vmem, vmem, pl.BlockSpec(memory_space=pl.ANY)] + [vmem] * 7
+        + [pl.BlockSpec(memory_space=pltpu.SMEM), vmem, vmem],
         out_specs=(vmem, vmem),
         scratch_shapes=[
+            pltpu.VMEM((1, width), F32),
             pltpu.VMEM((width, heads), BF16),
             pltpu.VMEM((rows, width), BF16),
             pltpu.VMEM((rows, 128), F32),
             pltpu.VMEM((rows, heads), F32),
             pltpu.VMEM((rows, heads), F32),
             pltpu.VMEM((ns, latent_width, crit_cols), F32),
-            pltpu.VMEM((ng, 2 * latent_width, crit_cols), BF16),
-            pltpu.VMEM((ng, crit_cols, latent_width), BF16),
-            pltpu.VMEM((ns, crit_rows, latent_width), BF16),
-            pltpu.VMEM((nt, rows, latent_width), BF16),
-            pltpu.VMEM((nt, rows, latent_width), BF16),
+            pltpu.VMEM((ng, crit_cols, 2 * latent_width), BF16),
+            pltpu.VMEM((ng, latent_width, crit_cols), BF16),
+            pltpu.VMEM((ns, latent_width, crit_rows), BF16),
+            pltpu.VMEM((nt, latent_width, rows), BF16),
+            pltpu.VMEM((nt, latent_width, rows), BF16),
             pltpu.VMEM((nt, 8, rows), F32),
-            pltpu.VMEM((nt - 1, rows, columns), BF16),
-            pltpu.VMEM((nt - 1, rows, columns), BF16),
-            pltpu.VMEM((nt - 1, rows, columns), BF16),
-            pltpu.VMEM((nt - 1, rows, columns), BF16),
+            pltpu.VMEM((nt - 1, HALVES, rows // HALVES, columns), BF16),
+            pltpu.VMEM((nt - 1, HALVES, rows // HALVES, columns), BF16),
+            pltpu.VMEM((nt - 1, HALVES, rows // HALVES, columns), BF16),
+            pltpu.VMEM((nt - 1, HALVES, rows // HALVES, columns), BF16),
             pltpu.VMEM((rows, columns), F32),
             dma,
             dma((ns - 1, pieces)),
@@ -426,18 +461,19 @@
             dma((ng - 1,)),
             dma((3, nt - 1)),
             dma((3, nt - 1)),
-            dma((nt - 1,)),
-            dma((nt - 1,)),
-            dma((nt - 1,)),
-            dma((nt - 1,)),
+            dma((nt - 1, HALVES)),
+            dma((nt - 1, HALVES)),
+            dma((nt - 1, HALVES)),
+            dma((nt - 1, HALVES)),
         ],
         compiler_params=pltpu.CompilerParams(
             collective_id=0, has_side_effects=True, vmem_limit_bytes=56 * 1024 * 1024
         ),
     )(
-        hidden, norm_gain.reshape(1, width), gen_value, gen_head, critic_embed, eg_pair,
-        critic_value, critic_head, noise, owner.reshape(rows, 1), coef,
+        hidden, norm_gain, gen_value, gen_head.T, critic_embed, scaling, critic_value.T, critic_head.T,
+        noise.T, owner, tsteps, noise_mix, gap_weight,
     )
+    return latent.T, grad
 
 
 def solution(mesh):

time: 121 us -> 95.2 us (0.79)
  local copies, waits for them, and re-layouts: 15.3 us -> 3.34 us
  Pallas kernels: 99.7 us -> 90.3 us
  other arithmetic: 3.99 us -> 0 us
    pallas_call x1, Pallas kernels: 99.7 us -> 90.3 us  [local(): pl.pallas_call(functools.partial(kernel, ng, ns, nt, shared, pieces), out...]
    unnamed x9 -> x2, local copies, waits for them, and re-layouts: 9.5 us -> 3.34 us
    reshape x2 -> x0, local copies, waits for them, and re-layouts: 2.79 us -> none  [the longest x1 1.47 us: local(): owner.reshape(rows, 1)]
    pallas_call x1 -> x0, local copies, waits for them, and re-layouts: 1.54 us -> none  [local(): pl.pallas_call(functools.partial(kernel, ng, ns, nt, shared, pieces), out...]
    dynamic_slice x2 -> x0, local copies, waits for them, and re-layouts: 1.46 us -> none  [the longest x1 1.27 us: local(): weight = lax.dynamic_index_in_dim(gap_weight, level, 0, keepdims=True)]
    reshape x1 -> x0, other arithmetic: 1.23 us -> none  [local(): coef = jnp.pad(jnp.concatenate([mix, weight]), (0, 125)).reshape(1, 128)]
where the time goes in v3:
time: 95.2 us; the launch traced here: 94.9 us
  Pallas kernels  90.3 us (95%)
  local copies, waits for them, and re-layouts  3.34 us (4%)
  between operations  1.29 us (1%)
    pallas_call x1, Pallas kernels, local(): pl.pallas_call(functools.partial(kernel, ng, ns, nt, shared, pieces), out...  90.3 us
    unnamed x2, local copies, waits for them, and re-layouts  3.34 us

profile of v3, /device:TPU:0, one launch (start us, length us, event | category | flops | bytes accessed | tf_op | source)
XLA Modules:
  0.0 94.9 jit_solution(15490924241826604831)
XLA Ops:
  1.3 90.3 %shard_map.140 = (bf16[64,256]{1,0:T(8,128)(2,1)}, bf16[256,1280]{1,0:T(8,128)(2,1)}) custom-call(bf16[256,5120]{1,0:T(8,128)(2,1)} %hidden.1, bf16[5120]{0:T(1024)(128)(2,1)} %gain_in.1, bf16[2560,640]{1,0:T(8,128)(2,1)} %weights.1, bf16[64,640]{1,0:T(8,128)(2,1)} %bitcast.7, bf16[2,64,5120]{2,1,0:T(8,128)(2,1)} %embed.1, bf16[2,5120]{1,0:T(2,128)(2,1)} %scaling.1, ...), custom_call_target="tpu_custom_call" | custom-call | tf_op jit(solution)/shard_map/pallas_call | solution.py:421
  91.6 1.4 %copy.18 = bf16[256,64]{0,1:T(8,128)(2,1)} copy(bf16[256,64]{0,1:T(8,128)(2,1)} %bitcast.9) | data formatting | bytes 65536
  93.0 2.0 %copy.19 = bf16[256,1280]{1,0:T(8,128)(2,1)} copy(bf16[256,1280]{1,0:T(8,128)(2,1)} %get-tuple-element.9) | data formatting | bytes 1310720

commit v4 on v3

--- a/solution.py
+++ b/solution.py
@@ -34,9 +34,9 @@
 
 def kernel(
     ng, ns, nt, shared, pieces,
-    hidden, gain_in, weights, gen_head, embed, scaling, crit_value, crit_head, noise, owner, tsteps, tables, weighting,
+    hidden_in, gain_in, weights, gen_head, embed_in, scaling, crit_value_in, crit_head, noise, owner, tsteps, tables, weighting,
     latent_out, grad_out,
-    gain, wall, normed, inv_ref, values, slope, mpart, mall, hall, noise_all, latp, gapp, inn,
+    hidden, embed, crit_value, load_sem, gain, wall, normed, inv_ref, values, slope, mpart, mall, hall, noise_all, latp, gapp, inn,
     send_r, send_l, recv_r, recv_l, total,
     own_sem, w_send, w_recv, f_send, f_recv, m_send, m_recv, n_send, n_recv,
     g_send, g_recv, h_send, h_recv, t_send, t_recv, rs_sem, rr_sem, ls_sem, lr_sem,
@@ -44,10 +44,10 @@
     g = lax.axis_index("group")
     s = lax.axis_index("seq")
     t = lax.axis_index("tp")
-    rows, width = hidden.shape
+    rows, width = hidden_in.shape
     depth = weights.shape[0]
     crit_rows = noise.shape[1]
-    channels = noise.shape[0]
+    half = channels = noise.shape[0]
     columns = width // nt
     pending = []
 
@@ -68,6 +68,11 @@
         copy.start()
         pending.append(copy)
         return copy
+
+    loads = []
+    for k, (src, dst) in enumerate(((hidden_in, hidden), (crit_value_in, crit_value), (embed_in, embed))):
+        loads.append(pltpu.make_async_copy(src, dst, load_sem.at[k]))
+        loads[-1].start()
 
     barrier = pltpu.get_barrier_semaphore()
     for o in range(1, ns):
@@ -91,10 +96,6 @@
                 wall.at[pl.ds(s * depth + mine + p * step, step), :],
                 w_send.at[o - 1, p], w_recv.at[o - 1, p], {"seq": seq_peer(o)},
             )
-    n_copies = [
-        push(noise, noise_all.at[s], n_send.at[o - 1], n_recv.at[o - 1], {"seq": seq_peer(o)})
-        for o in range(1, ns)
-    ]
     h_copies = [
         push(crit_head, hall.at[g], h_send.at[o - 1], h_recv.at[o - 1], {"group": group_peer(o)})
         for o in range(1, ng)
@@ -102,64 +103,84 @@
     noise_all[s] = noise[...]
     hall[g] = crit_head[...]
 
-    half = channels
-    if depth % 128 == 0:
-        critic = g // (ng // 2)
-        at = pl.ds(pl.multiple_of(s * depth, 128), depth)
-        both = scaling[:, at].astype(F32)
-        eg = embed[critic, :, at].astype(F32) * jnp.where(critic == 0, both[0:1], both[1:2])
-        eg_high = eg.astype(BF16)
-        eg_low = (eg - eg_high.astype(F32)).astype(BF16)
-        eg_pair = jnp.concatenate([eg_high, eg_low], axis=0)
-    else:
-        eg_pair = scaling[...]
-    folded = dot_t(eg_pair, crit_value[...])
-    mpart[s] = folded[:half] + folded[half:]
+    def fold():
+        if depth % 128 == 0:
+            critic = g // (ng // 2)
+            at = pl.ds(pl.multiple_of(s * depth, 128), depth)
+            both = scaling[:, at].astype(F32)
+            eg = embed[critic, :, at].astype(F32) * jnp.where(critic == 0, both[0:1], both[1:2])
+            eg_high = eg.astype(BF16)
+            eg_low = (eg - eg_high.astype(F32)).astype(BF16)
+            eg_pair = jnp.concatenate([eg_high, eg_low], axis=0)
+        else:
+            eg_pair = scaling[...]
+        folded = dot_t(eg_pair, crit_value[...])
+        mpart[s] = folded[:half] + folded[half:]
+
+    def norm_all():
+        gain[...] = gain_in[...].astype(F32).reshape(1, width)
+
+        def norm_rows(r, carry):
+            at = pl.ds(pl.multiple_of(r * 32, 32), 32)
+            x = hidden[at, :].astype(F32)
+            inverse = lax.rsqrt(jnp.mean(x * x, axis=-1, keepdims=True) + 1e-06)
+            normed[at, :] = (x * inverse * gain[...]).astype(BF16)
+            inv_ref[at, :] = jnp.broadcast_to(inverse, (32, 128))
+            return carry
+
+        lax.fori_loop(0, rows // 32, norm_rows, 0)
+        values[...] = jnp.zeros_like(values)
+
+    def add_rows(start, size):
+        at = pl.multiple_of(start, 128)
+        values[...] += dot(normed[:, pl.ds(at, size)], wall[pl.ds(at, size), :])
+
+    def own_rows(j, carry):
+        add_rows(s * depth + j * quarter, quarter)
+        return carry
+
+    x_copies, c_copies, d_copies = {}, {}, {}
+
+    def forward(p):
+        for o in range(1, ns):
+            w_copies[o, p].wait_recv()
+            base = lax.rem(s - o + ns, ns) * depth
+            at = pl.ds(base + mine + p * step, step)
+            x_copies[o, p] = push(
+                wall.at[at, :], wall.at[at, :],
+                f_send.at[0, o - 1, p], f_recv.at[0, o - 1, p], {"group": g ^ 2},
+            )
+            c_copies[o, p] = push(
+                wall.at[at, :], wall.at[at, :],
+                f_send.at[1, o - 1, p], f_recv.at[1, o - 1, p], {"group": g ^ 1},
+            )
+
+    if shared:
+        forward(0)
+    loads[0].wait()
+    norm_all()
+    if shared:
+        forward(1)
+        forward(2)
+    local.wait()
+    if shared:
+        lax.fori_loop(0, ng, own_rows, 0)
+        forward(3)
+    loads[1].wait()
+    loads[2].wait()
+    fold()
+    if shared:
+        for p in range(4, pieces):
+            forward(p)
+    n_copies = [
+        push(noise, noise_all.at[s], n_send.at[o - 1], n_recv.at[o - 1], {"seq": seq_peer(o)})
+        for o in range(1, ns)
+    ]
     m_copies = [
         push(mpart.at[s], mpart.at[s], m_send.at[o - 1], m_recv.at[o - 1], {"seq": seq_peer(o)})
         for o in range(1, ns)
     ]
-
-    gain[...] = gain_in[...].astype(F32).reshape(1, width)
-
-    def norm_rows(r, carry):
-        at = pl.ds(pl.multiple_of(r * 32, 32), 32)
-        x = hidden[at, :].astype(F32)
-        inverse = lax.rsqrt(jnp.mean(x * x, axis=-1, keepdims=True) + 1e-06)
-        normed[at, :] = (x * inverse * gain[...]).astype(BF16)
-        inv_ref[at, :] = jnp.broadcast_to(inverse, (32, 128))
-        return carry
-
-    lax.fori_loop(0, rows // 32, norm_rows, 0)
-    values[...] = jnp.zeros_like(values)
-
-    def add_rows(start, size):
-        at = pl.multiple_of(start, 128)
-        values[...] += dot(normed[:, pl.ds(at, size)], wall[pl.ds(at, size), :])
-
     if shared:
-        x_copies, c_copies, d_copies = {}, {}, {}
-        for p in range(pieces):
-            for o in range(1, ns):
-                w_copies[o, p].wait_recv()
-                base = lax.rem(s - o + ns, ns) * depth
-                at = pl.ds(base + mine + p * step, step)
-                x_copies[o, p] = push(
-                    wall.at[at, :], wall.at[at, :],
-                    f_send.at[0, o - 1, p], f_recv.at[0, o - 1, p], {"group": g ^ 2},
-                )
-                c_copies[o, p] = push(
-                    wall.at[at, :], wall.at[at, :],
-                    f_send.at[1, o - 1, p], f_recv.at[1, o - 1, p], {"group": g ^ 1},
-                )
-            if p == 0:
-                local.wait()
-
-                def own_rows(j, carry):
-                    add_rows(s * depth + j * quarter, quarter)
-                    return carry
-
-                lax.fori_loop(0, ng, own_rows, 0)
         for p in range(pieces):
             for o in range(1, ns):
                 x_copies[o, p].wait_recv()
@@ -169,8 +190,6 @@
                     wall.at[at, :], wall.at[at, :],
                     f_send.at[2, o - 1, p], f_recv.at[2, o - 1, p], {"group": g ^ 1},
                 )
-    else:
-        local.wait()
 
     for copy in m_copies:
         copy.wait_recv()
@@ -416,6 +435,7 @@
     shared = ng == 4 and depth % (128 * ng) == 0
     pieces = 8 if shared else 1
     vmem = pl.BlockSpec(memory_space=pltpu.VMEM)
+    far = pl.BlockSpec(memory_space=pl.ANY)
     columns = width // nt
     dma = pltpu.SemaphoreType.DMA
     latent, grad = pl.pallas_call(
@@ -424,10 +444,14 @@
             jax.ShapeDtypeStruct((latent_width, rows), BF16),
             jax.ShapeDtypeStruct((rows, columns), BF16),
         ),
-        in_specs=[vmem, vmem, pl.BlockSpec(memory_space=pl.ANY)] + [vmem] * 7
+        in_specs=[far, vmem, far, vmem, far, vmem, far] + [vmem] * 3
         + [pl.BlockSpec(memory_space=pltpu.SMEM), vmem, vmem],
         out_specs=(vmem, vmem),
         scratch_shapes=[
+            pltpu.VMEM((rows, width), BF16),
+            pltpu.VMEM(critic_embed.shape, BF16),
+            pltpu.VMEM((crit_cols, depth), BF16),
+            dma((3,)),
             pltpu.VMEM((1, width), F32),
             pltpu.VMEM((width, heads), BF16),
             pltpu.VMEM((rows, width), BF16),

time: 95.2 us -> 93.7 us (0.984)
  Pallas kernels: 90.3 us -> 88.8 us
    pallas_call x1, Pallas kernels: 90.3 us -> 88.8 us  [local(): pl.pallas_call(functools.partial(kernel, ng, ns, nt, shared, pieces), out...]
where the time goes in v4:
time: 93.7 us; the launch traced here: 93.5 us
  Pallas kernels  88.8 us (95%)
  local copies, waits for them, and re-layouts  3.34 us (4%)
  between operations  1.29 us (1%)
    pallas_call x1, Pallas kernels, local(): pl.pallas_call(functools.partial(kernel, ng, ns, nt, shared, pieces), out...  88.8 us
    unnamed x2, local copies, waits for them, and re-layouts  3.34 us

profile of v4, /device:TPU:0, one launch (start us, length us, event | category | flops | bytes accessed | tf_op | source)
XLA Modules:
  0.0 93.5 jit_solution(12768800382904627392)
XLA Ops:
  1.3 88.8 %shard_map.140 = (bf16[64,256]{1,0:T(8,128)(2,1)}, bf16[256,1280]{1,0:T(8,128)(2,1)}) custom-call(bf16[256,5120]{1,0:T(8,128)(2,1)} %hidden_in.1, bf16[5120]{0:T(1024)(128)(2,1)} %gain_in.1, bf16[2560,640]{1,0:T(8,128)(2,1)} %weights.1, bf16[64,640]{1,0:T(8,128)(2,1)} %bitcast.7, bf16[2,64,5120]{2,1,0:T(8,128)(2,1)} %embed_in.1, bf16[2,5120]{1,0:T(2,128)(2,1)} %scaling.1, ...), custom_call_target="tpu_custom_call" | custom-call | tf_op jit(solution)/shard_map/pallas_call | solution.py:441
  90.1 1.4 %copy.18 = bf16[256,64]{0,1:T(8,128)(2,1)} copy(bf16[256,64]{0,1:T(8,128)(2,1)} %bitcast.9) | data formatting | bytes 65536
  91.5 2.0 %copy.19 = bf16[256,1280]{1,0:T(8,128)(2,1)} copy(bf16[256,1280]{1,0:T(8,128)(2,1)} %get-tuple-element.9) | data formatting | bytes 1310720

commit v5 on v4

--- a/solution.py
+++ b/solution.py
@@ -38,6 +38,7 @@
     latent_out, grad_out,
     hidden, embed, crit_value, load_sem, gain, wall, normed, inv_ref, values, slope, mpart, mall, hall, noise_all, latp, gapp, inn,
     send_r, send_l, recv_r, recv_l, total,
+    wextra, gv_ref, gv_far, z_send, z_recv, zc_sem, gv_sem,
     own_sem, w_send, w_recv, f_send, f_recv, m_send, m_recv, n_send, n_recv,
     g_send, g_recv, h_send, h_recv, t_send, t_recv, rs_sem, rr_sem, ls_sem, lr_sem,
 ):
@@ -88,6 +89,25 @@
     quarter = depth // ng if shared else depth
     step = quarter // pieces
     mine = g * quarter if shared else 0
+    near = shared and nt == 4 and ns == 2 and 2 * quarter == columns
+    edge = jnp.logical_or(t == 0, t == nt - 1)
+    middle = jnp.logical_not(edge)
+    inward = {"tp": jnp.where(t == 0, 1, nt - 2)}
+    odd = lax.rem(g, 2)
+    want_half = jnp.where(t == 0, 0, 1)
+    want_quarter = jnp.where(t == 0, 2, 0) + odd
+
+    def hand(src, p):
+        return pltpu.make_async_remote_copy(
+            src_ref=src, dst_ref=wextra.at[pl.ds(odd * quarter + p * step, step), :],
+            send_sem=z_send.at[p], recv_sem=z_recv.at[p], device_id=inward, device_id_type=MESH,
+        )
+
+    def hand_far(p, index):
+        @pl.when(jnp.logical_and(edge, jnp.logical_and(s != want_half, want_quarter == index)))
+        def _():
+            hand(wall.at[pl.ds((1 - s) * depth + index * quarter + p * step, step), :], p).start()
+
     w_copies = {}
     for p in range(pieces):
         for o in range(1, ns):
@@ -96,6 +116,12 @@
                 wall.at[pl.ds(s * depth + mine + p * step, step), :],
                 w_send.at[o - 1, p], w_recv.at[o - 1, p], {"seq": seq_peer(o)},
             )
+    if near:
+        @pl.when(jnp.logical_and(edge, s == want_half))
+        def _():
+            for p in range(pieces):
+                hand(weights.at[pl.ds(want_quarter * quarter + p * step, step), :], p).start()
+
     h_copies = [
         push(crit_head, hall.at[g], h_send.at[o - 1], h_recv.at[o - 1], {"group": group_peer(o)})
         for o in range(1, ng)
@@ -154,6 +180,8 @@
                 wall.at[at, :], wall.at[at, :],
                 f_send.at[1, o - 1, p], f_recv.at[1, o - 1, p], {"group": g ^ 1},
             )
+        if near:
+            hand_far(p, g)
 
     if shared:
         forward(0)
@@ -190,6 +218,8 @@
                     wall.at[at, :], wall.at[at, :],
                     f_send.at[2, o - 1, p], f_recv.at[2, o - 1, p], {"group": g ^ 1},
                 )
+            if near:
+                hand_far(p, g ^ 2)
 
     for copy in m_copies:
         copy.wait_recv()
@@ -303,6 +333,24 @@
     inn[t] = jnp.broadcast_to(inner, (rows, 128)).T[:8]
     inn_copies = share_tp(inn, 2)
 
+    if near:
+        gv_ref[...] = grad_values
+    mate_rows = wextra.at[pl.ds(odd * quarter, quarter), :] if near else wextra
+    mate = pltpu.make_async_remote_copy(
+        src_ref=mate_rows, dst_ref=mate_rows, send_sem=zc_sem.at[0], recv_sem=zc_sem.at[1],
+        device_id={"group": g ^ 1}, device_id_type=MESH,
+    )
+    give = pltpu.make_async_remote_copy(
+        src_ref=gv_ref, dst_ref=gv_far, send_sem=gv_sem.at[0], recv_sem=gv_sem.at[1],
+        device_id=inward, device_id_type=MESH,
+    )
+    if near:
+        @pl.when(middle)
+        def _():
+            for p in range(pieces):
+                hand(wextra.at[pl.ds(odd * quarter + p * step, step), :], p).wait_recv()
+            mate.start()
+
     block = 256 if columns % 256 == 0 else columns
     part_rows = rows // HALVES
 
@@ -344,8 +392,13 @@
             if d < nt - 1:
                 @pl.when(starts)
                 def _():
-                    part(target, h, buf_s.at[d - 1, h], None)
-                    link(d, h).wait_send()
+                    if near and d == 1:
+                        link(d, h).wait_send()
+                        if h == HALVES - 1:
+                            give.start()
+                    else:
+                        part(target, h, buf_s.at[d - 1, h], None)
+                        link(d, h).wait_send()
 
                 @pl.when(jnp.logical_not(starts))
                 def _():
@@ -357,18 +410,25 @@
                             link(d, h).wait_send()
             else:
                 part(target, h, buf_s.at[d - 1, h], None)
-            link(d - 1, h).start()
+            if near and d == 1:
+                @pl.when(jnp.logical_not(starts))
+                def _():
+                    link(d - 1, h).start()
+            else:
+                link(d - 1, h).start()
 
     def chain_end(h, to_right):
         buf_s, buf_r, link = linker(to_right)
         at = pl.ds(h * part_rows, part_rows)
 
-        @pl.when(t > 0 if to_right else t < nt - 1)
+        skip = 1 if near else 0
+
+        @pl.when(t > skip if to_right else t < nt - 1 - skip)
         def _():
             link(0, h).wait_recv()
             total[at, :] += buf_r[0, h].astype(F32)
 
-        @pl.when(t < nt - 1 if to_right else t > 0)
+        @pl.when(middle if near else (t < nt - 1 if to_right else t > 0))
         def _():
             link(0, h).wait_send()
 
@@ -383,6 +443,26 @@
     for h in range(HALVES):
         chain_end(h, True)
         chain_end(h, False)
+    if near:
+        @pl.when(middle)
+        def _():
+            mate.wait_recv()
+            give.wait_recv()
+
+            def near_part(j, carry):
+                at = pl.ds(pl.multiple_of(j * block, block), block)
+                total[:, at] += dot_t(gv_far[...], wextra[at, :])
+                return carry
+
+            lax.fori_loop(0, columns // block, near_part, 0)
+            mate.wait_send()
+
+        @pl.when(edge)
+        def _():
+            give.wait_send()
+            for p in range(pieces):
+                hand(wextra.at[pl.ds(odd * quarter + p * step, step), :], p).wait_send()
+
     inverse = inv_ref[:, :1]
     mixed = inner_col / (inverse * width)
     factor = inverse * inverse * inverse * mixed
@@ -470,6 +550,13 @@
             pltpu.VMEM((nt - 1, HALVES, rows // HALVES, columns), BF16),
             pltpu.VMEM((nt - 1, HALVES, rows // HALVES, columns), BF16),
             pltpu.VMEM((rows, columns), F32),
+            pltpu.VMEM((columns, heads), BF16),
+            pltpu.VMEM((rows, heads), BF16),
+            pltpu.VMEM((rows, heads), BF16),
+            dma((pieces,)),
+            dma((pieces,)),
+            dma((2,)),
+            dma((2,)),
             dma,
             dma((ns - 1, pieces)),
             dma((ns - 1, pieces)),

time: 93.7 us -> 99.7 us (1.064)
  the two profiles are of different devices: /device:TPU:0 before, /device:TPU:10 now
where the time goes in v5:
time: 99.7 us; the launch traced here: 99.5 us
  Pallas kernels  94.9 us (95%)
  local copies, waits for them, and re-layouts  3.34 us (3%)
  between operations  1.29 us (1%)
    pallas_call x1, Pallas kernels, local(): pl.pallas_call(functools.partial(kernel, ng, ns, nt, shared, pieces), out...  94.9 us
    unnamed x2, local copies, waits for them, and re-layouts  3.34 us

profile of v5, /device:TPU:10, one launch (start us, length us, event | category | flops | bytes accessed | tf_op | source)
XLA Modules:
  0.0 99.5 jit_solution(12775336958120023154)
XLA Ops:
  1.3 94.9 %shard_map.140 = (bf16[64,256]{1,0:T(8,128)(2,1)}, bf16[256,1280]{1,0:T(8,128)(2,1)}) custom-call(bf16[256,5120]{1,0:T(8,128)(2,1)} %hidden_in.1, bf16[5120]{0:T(1024)(128)(2,1)} %gain_in.1, bf16[2560,640]{1,0:T(8,128)(2,1)} %weights.1, bf16[64,640]{1,0:T(8,128)(2,1)} %bitcast.7, bf16[2,64,5120]{2,1,0:T(8,128)(2,1)} %embed_in.1, bf16[2,5120]{1,0:T(2,128)(2,1)} %scaling.1, ...), custom_call_target="tpu_custom_call" | custom-call | tf_op jit(solution)/shard_map/pallas_call | solution.py:521
  96.1 1.4 %copy.18 = bf16[256,64]{0,1:T(8,128)(2,1)} copy(bf16[256,64]{0,1:T(8,128)(2,1)} %bitcast.9) | data formatting | bytes 65536
  97.5 2.0 %copy.19 = bf16[256,1280]{1,0:T(8,128)(2,1)} copy(bf16[256,1280]{1,0:T(8,128)(2,1)} %get-tuple-element.9) | data formatting | bytes 1310720

commit v6 on v4

--- a/solution.py
+++ b/solution.py
@@ -38,7 +38,7 @@
     latent_out, grad_out,
     hidden, embed, crit_value, load_sem, gain, wall, normed, inv_ref, values, slope, mpart, mall, hall, noise_all, latp, gapp, inn,
     send_r, send_l, recv_r, recv_l, total,
-    own_sem, w_send, w_recv, f_send, f_recv, m_send, m_recv, n_send, n_recv,
+    own_part, own_sem, w_send, w_recv, f_send, f_recv, m_send, m_recv, n_send, n_recv,
     g_send, g_recv, h_send, h_recv, t_send, t_recv, rs_sem, rr_sem, ls_sem, lr_sem,
 ):
     g = lax.axis_index("group")
@@ -306,15 +306,13 @@
     block = 256 if columns % 256 == 0 else columns
     part_rows = rows // HALVES
 
-    def part(q, h, out, extra):
+    def part(q, h, out):
         lhs = grad_values[h * part_rows:(h + 1) * part_rows]
 
         def one(j, carry):
             at = pl.ds(pl.multiple_of(j * block, block), block)
             w = wall[pl.ds(pl.multiple_of(q * columns + j * block, block), block), :]
             term = dot_t(lhs, w)
-            if extra is not None:
-                term = term + extra[:, at].astype(F32)
             out[:, at] = term.astype(out.dtype)
             return carry
 
@@ -344,19 +342,20 @@
             if d < nt - 1:
                 @pl.when(starts)
                 def _():
-                    part(target, h, buf_s.at[d - 1, h], None)
+                    part(target, h, buf_s.at[d - 1, h])
                     link(d, h).wait_send()
 
                 @pl.when(jnp.logical_not(starts))
                 def _():
+                    part(target, h, own_part)
                     link(d, h).wait_recv()
-                    part(target, h, buf_s.at[d - 1, h], buf_r.at[d, h])
+                    buf_s[d - 1, h] = (own_part[...] + buf_r[d, h].astype(F32)).astype(BF16)
                     if d < nt - 2:
                         @pl.when(further)
                         def _():
                             link(d, h).wait_send()
             else:
-                part(target, h, buf_s.at[d - 1, h], None)
+                part(target, h, buf_s.at[d - 1, h])
             link(d - 1, h).start()
 
     def chain_end(h, to_right):
@@ -377,7 +376,7 @@
             chain(d, h, True)
             chain(d, h, False)
     for h in range(HALVES):
-        part(t, h, total.at[pl.ds(h * part_rows, part_rows), :], None)
+        part(t, h, total.at[pl.ds(h * part_rows, part_rows), :])
     inner_all = sum_tp(inn, inn_copies)
     inner_col = jnp.broadcast_to(inner_all[0:1], (128, rows)).T[:, :1]
     for h in range(HALVES):
@@ -470,6 +469,7 @@
             pltpu.VMEM((nt - 1, HALVES, rows // HALVES, columns), BF16),
             pltpu.VMEM((nt - 1, HALVES, rows // HALVES, columns), BF16),
             pltpu.VMEM((rows, columns), F32),
+            pltpu.VMEM((rows // HALVES, columns), F32),
             dma,
             dma((ns - 1, pieces)),
             dma((ns - 1, pieces)),

time: 93.7 us -> 93.7 us (level)
  no operation moved by 1% of the time
where the time goes in v6:
time: 93.7 us; the launch traced here: 93.5 us
  Pallas kernels  88.8 us (95%)
  local copies, waits for them, and re-layouts  3.34 us (4%)
  between operations  1.29 us (1%)
    pallas_call x1, Pallas kernels, local(): pl.pallas_call(functools.partial(kernel, ng, ns, nt, shared, pieces), out...  88.8 us
    unnamed x2, local copies, waits for them, and re-layouts  3.34 us

profile of v6, /device:TPU:0, one launch (start us, length us, event | category | flops | bytes accessed | tf_op | source)
XLA Modules:
  0.0 93.5 jit_solution(7758237100509261339)
XLA Ops:
  1.3 88.8 %shard_map.140 = (bf16[64,256]{1,0:T(8,128)(2,1)}, bf16[256,1280]{1,0:T(8,128)(2,1)}) custom-call(bf16[256,5120]{1,0:T(8,128)(2,1)} %hidden_in.1, bf16[5120]{0:T(1024)(128)(2,1)} %gain_in.1, bf16[2560,640]{1,0:T(8,128)(2,1)} %weights.1, bf16[64,640]{1,0:T(8,128)(2,1)} %bitcast.7, bf16[2,64,5120]{2,1,0:T(8,128)(2,1)} %embed_in.1, bf16[2,5120]{1,0:T(2,128)(2,1)} %scaling.1, ...), custom_call_target="tpu_custom_call" | custom-call | tf_op jit(solution)/shard_map/pallas_call | solution.py:440
  90.1 1.4 %copy.18 = bf16[256,64]{0,1:T(8,128)(2,1)} copy(bf16[256,64]{0,1:T(8,128)(2,1)} %bitcast.9) | data formatting | bytes 65536
  91.5 2.0 %copy.19 = bf16[256,1280]{1,0:T(8,128)(2,1)} copy(bf16[256,1280]{1,0:T(8,128)(2,1)} %get-tuple-element.9) | data formatting | bytes 1310720
